TPU v7x, 128 devices: a whole 4x4x4 slice. The times are simulated.
128 devices in a mesh: seq: 16 (over y, x), ret: 8 (over z, core).
Axes of the slice: x: 4, y: 4, z: 4, core: 2. Of those that a mesh axis runs over, the one named last changes fastest.
Arguments:
- queries: bfloat16 [12288, 4096], P('seq', 'ret'), may hold values from -4 to 4
- grad_ctx: bfloat16 [12288, 4096], P('seq', 'ret'), may hold values from -6 to 6
- neighbours: bfloat16 [256, 128, 896], P(('seq', 'ret')), may hold values from -6 to 6
- up_weight: bfloat16 [896, 3584], replicated, may hold values from -0.1875 to 0.1875
- down_weight: bfloat16 [3584, 896], replicated, may hold values from -0.09375 to 0.09375
- key_weight: bfloat16 [896, 4096], P(None, 'ret'), may hold values from -0.1875 to 0.1875
- value_weight: bfloat16 [896, 4096], P(None, 'ret'), may hold values from -0.1875 to 0.1875
- group_ids: int32 [192, 2], P('seq'), may hold values from 0 to 15, all different within a row; in each aligned block of 12 rows (0 to 11, 12 to 23, ...) at most 3 rows name the same one
- slot_ids: int32 [192, 2], P('seq'), may hold values from 0 to 15
Outputs:
- context: bfloat16 [12288, 4096], P('seq', 'ret')
- grad_queries: bfloat16 [12288, 4096], P('seq', 'ret')
- grad_encoded: bfloat16 [256, 128, 896], P(('seq', 'ret'))
- grad_key_weight: float32 [896, 4096], P('seq', 'ret')
- grad_value_weight: float32 [896, 4096], P('seq', 'ret')
Inputs may be any that keep to these rules, and one draw needn't show every extreme that they name: `group_ids`: the two neighbours of a span lie on different indices of seq. Among the spans of one index of seq no index of seq is named more than 3 times, and in every draw some index of seq is named exactly 3 times by the spans of some index of seq.
All inputs are finite; a program needn't handle non-finite values.
Results may differ from a plain program's by a relative error of at most 0.018.
Values may be sent and summed in bfloat16 or wider, within the bound.
A program may use at most 192 MiB of HBM per device.

v0:
```python
import math

import jax
import jax.numpy as jnp
from jax import lax
from jax.sharding import PartitionSpec as P

HD = 128


def encode(raw_block, up_weight, down_weight):
    amount, row_len, feat_width = raw_block.shape
    inputs = raw_block.reshape(-1, feat_width).astype(jnp.float32)
    normed = (inputs * lax.rsqrt(jnp.mean(inputs * inputs, axis=-1, keepdims=True) + 1e-06)).astype(
        jnp.bfloat16
    )
    hidden = jax.nn.gelu(jnp.dot(normed, up_weight, preferred_element_type=jnp.float32)).astype(
        jnp.bfloat16
    )
    output = inputs + jnp.dot(hidden, down_weight, preferred_element_type=jnp.float32)
    return output.astype(jnp.bfloat16).reshape(amount, row_len, feat_width)


def attend(queries, key_req, value_req, grad_out):
    score_scale = 1.0 / math.sqrt(queries.shape[-1])
    scores = (
        jnp.einsum("cqhd,ckhd->chqk", queries, key_req, preferred_element_type=jnp.float32)
        * score_scale
    )
    weights = jnp.exp(scores)
    weights = weights / jnp.sum(weights, axis=-1, keepdims=True)
    probs = weights.astype(jnp.bfloat16)
    context = jnp.einsum(
        "chqk,ckhd->cqhd", probs, value_req, preferred_element_type=jnp.float32
    ).astype(jnp.bfloat16)
    grad_probs = jnp.einsum(
        "cqhd,ckhd->chqk", grad_out, value_req, preferred_element_type=jnp.float32
    )
    mixed = (
        weights * (grad_probs - jnp.sum(weights * grad_probs, axis=-1, keepdims=True)) * score_scale
    ).astype(jnp.bfloat16)
    grad_queries = jnp.einsum(
        "chqk,ckhd->cqhd", mixed, key_req, preferred_element_type=jnp.float32
    ).astype(jnp.bfloat16)
    grad_keys = jnp.einsum(
        "chqk,cqhd->ckhd", mixed, queries, preferred_element_type=jnp.float32
    ).astype(jnp.bfloat16)
    grad_values = jnp.einsum(
        "chqk,cqhd->ckhd", probs, grad_out, preferred_element_type=jnp.float32
    ).astype(jnp.bfloat16)
    return (context, grad_queries, grad_keys, grad_values)


def full_table(encoded_own):
    return lax.all_gather(encoded_own, "ret", axis=0, tiled=True)


def home_sum(returned, served, table_len, row_len, feat_width):
    selector = (served[:, None] == jnp.arange(table_len, dtype=jnp.int32)[None, :]).astype(
        jnp.bfloat16
    )
    table_grad = jnp.einsum("ns,nx->sx", selector, returned, preferred_element_type=jnp.float32)
    table_grad = table_grad.reshape(table_len, row_len, feat_width)
    return lax.psum_scatter(table_grad, "ret", scatter_dimension=0, tiled=True).astype(jnp.bfloat16)


def body(
    queries,
    grad_ctx,
    neighbours,
    up_weight,
    down_weight,
    key_weight,
    value_weight,
    group_ids,
    slot_ids,
):
    groups = lax.axis_size("seq")
    span_count = group_ids.shape[0]
    capacity = 2 * span_count // groups + 2
    slot_total = groups * capacity
    head_width = queries.shape[1]
    block_heads = head_width // HD
    span_len = queries.shape[0] // span_count
    encoded_own = encode(neighbours, up_weight, down_weight)
    own_count, row_len, feat_width = encoded_own.shape
    table_len = own_count * lax.axis_size("ret")
    targets = group_ids.reshape(-1)
    slot_list = slot_ids.reshape(-1)
    requests = targets.shape[0]
    one_hot = (targets[:, None] == jnp.arange(groups, dtype=jnp.int32)[None, :]).astype(jnp.int32)
    before = jnp.cumsum(one_hot, axis=0) - one_hot
    position = targets * capacity + jnp.sum(before * one_hot, axis=1)
    wanted = jnp.zeros((slot_total,), jnp.int32).at[position].set(slot_list)
    served = lax.all_to_all(
        wanted.reshape(groups, capacity), "seq", split_axis=0, concat_axis=0, tiled=True
    ).reshape(-1)
    enc_table = full_table(encoded_own)
    source_rows = jnp.take(enc_table, served, axis=0)
    arrived = lax.all_to_all(
        source_rows.reshape(groups, capacity, row_len, feat_width),
        "seq",
        split_axis=0,
        concat_axis=0,
        tiled=True,
    )
    picked = jnp.take(arrived.reshape(slot_total, row_len, feat_width), position, axis=0).reshape(
        -1, feat_width
    )
    key_flat = jnp.dot(picked, key_weight, preferred_element_type=jnp.float32).astype(jnp.bfloat16)
    value_flat = jnp.dot(picked, value_weight, preferred_element_type=jnp.float32).astype(
        jnp.bfloat16
    )
    shape_q = (span_count, span_len, block_heads, HD)
    shape_kv = (span_count, 2 * row_len, block_heads, HD)
    context, grad_query, grad_keys, grad_values = attend(
        queries.reshape(shape_q),
        key_flat.reshape(shape_kv),
        value_flat.reshape(shape_kv),
        grad_ctx.reshape(shape_q),
    )
    grad_keys = grad_keys.reshape(-1, head_width)
    grad_values = grad_values.reshape(-1, head_width)
    grad_key_w = jnp.einsum("rd,rh->dh", picked, grad_keys, preferred_element_type=jnp.float32)
    grad_value_w = jnp.einsum("rd,rh->dh", picked, grad_values, preferred_element_type=jnp.float32)
    grad_part = (
        jnp.dot(grad_keys, key_weight.T, preferred_element_type=jnp.float32)
        + jnp.dot(grad_values, value_weight.T, preferred_element_type=jnp.float32)
    ).astype(jnp.bfloat16)
    placed = (
        jnp.zeros((slot_total, row_len * feat_width), jnp.bfloat16)
        .at[position]
        .set(grad_part.reshape(requests, -1))
    )
    returned = lax.all_to_all(
        placed.reshape(groups, capacity, row_len * feat_width),
        "seq",
        split_axis=0,
        concat_axis=0,
        tiled=True,
    )
    returned = returned.reshape(slot_total, -1)
    grad_encoded = home_sum(returned, served, table_len, row_len, feat_width)
    grad_key_out, grad_value_out = (
        lax.psum_scatter(grad_key_w, "seq", scatter_dimension=0, tiled=True),
        lax.psum_scatter(grad_value_w, "seq", scatter_dimension=0, tiled=True),
    )
    return (
        context.reshape(-1, head_width),
        grad_query.reshape(-1, head_width),
        grad_encoded,
        grad_key_out,
        grad_value_out,
    )


def solution(mesh):
    return jax.shard_map(
        body,
        mesh=mesh,
        in_specs=(
            P("seq", "ret"),
            P("seq", "ret"),
            P(("seq", "ret"), None, None),
            P(),
            P(),
            P(None, "ret"),
            P(None, "ret"),
            P("seq", None),
            P("seq", None),
        ),
        out_specs=(
            P("seq", "ret"),
            P("seq", "ret"),
            P(("seq", "ret"), None, None),
            P("seq", "ret"),
            P("seq", "ret"),
        ),
        check_vma=False,
    )
```

profile of v0, /device:TPU:1, one launch (start us, length us, event | category | flops | bytes accessed | tf_op | source)
XLA Modules:
  0.0 923.1 jit_solution(9724407605302720251)
XLA Ops:
  9.7 9.5 %fusion.56 = bf16[256,896]{1,0:T(8,128)(2,1)} fusion(bf16[3584,896]{1,0:T(8,128)(2,1)} %param.13, bf16[256,896]{1,0:T(8,128)(2,1)S(1)} %fusion.59, bf16[896,3584]{1,0:T(8,128)(2,1)} %param.12, bf16[256,896]{1,0:T(8,128)(2,1)} %bitcast.140), kind=kOutput, calls=%fused_computation.63 | convolution fusion | flops 3297280000 | bytes 14221312 | tf_op jit(solution)/shard_map/dot_general | solution.py:20
  20.9 13.8 %all_to_all.19 = s32[16,1,3]{2,1,0:T(1,128)S(1)} all-to-all(s32[16,1,3]{2,1,0:T(1,128)S(1)} %bitcast.143), channel_id=1, replica_groups=mesh['seq'=16,'ret'=8] {'seq'}, dimensions={0} | all-to-all | bytes 384 | tf_op jit(solution)/shard_map/all_to_all | solution.py:95
  36.1 17.0 %all-gather.2.cloned.1.call-done = bf16[16,128,896]{2,1,0:T(8,128)(2,1)} async-done(((bf16[2,128,896]{2,1,0:T(8,128)(2,1)}), bf16[16,128,896]{2,1,0:T(8,128)(2,1)}) %all-gather.2.cloned.1.call-update) | async-done | bytes 3670032 | tf_op jit(solution)/shard_map/all_gather | solution.py:55
  53.2 9.3 %gather_fusion = bf16[48,128,896]{2,1,0:T(8,128)(2,1)} fusion(bf16[16,128,896]{2,1,0:T(8,128)(2,1)} %all-gather.2.cloned.1.call-done, s32[1024]{0:T(1024)S(1)} %pad_clamp_fusion.1), kind=kCustom, calls=%fused_computation | custom fusion | bytes 22020288 | tf_op jit(solution)/shard_map/jit(_take)/gather | solution.py:99
  62.4 10.0 %broadcast_select_fusion = bf16[16,3,128,896]{3,2,1,0:T(8,128)(2,1)} fusion(bf16[16,3,128,896]{3,2,1,0:T(8,128)(2,1)} %bitcast.130, pred[16,3]{1,0:T(8,128)(4,1)S(1)} %copy.52), kind=kLoop, calls=%fused_computation.9 | loop fusion | flops 5505024 | bytes 22020144 | tf_op jit(solution)/shard_map/jit(_take)/select_n | solution.py:99
  72.4 7.2 all-to-all-start.1
  80.1 163.8 %all-to-all-done.1 = bf16[16,3,128,896]{3,2,1,0:T(8,128)(2,1)} async-done(((bf16[16,3,128,896]{3,2,1,0:T(8,128)(2,1)}), bf16[16,3,128,896]{3,2,1,0:T(8,128)(2,1)}, u32[]{:S(2)}, u32[]{:S(2)}) %all-to-all-start.1) | async-done | bytes 11010080 | tf_op jit(solution)/shard_map/all_to_all | solution.py:100
  243.9 8.0 gather_fusion.1
  251.9 3.7 bitcast_select_fusion
  255.6 4.8 convolution_convert_fusion
  260.4 4.8 convolution_convert_fusion.1
  265.2 5.5 reshape.231
  270.7 5.5 reshape.232
  276.1 4.9 fusion.26
  287.4 24.5 %convert_bitcast_fusion.1 = bf16[12,256,4,128]{3,1,2,0:T(8,128)(2,1)} fusion(f32[12,4,256,64]{2,3,1,0:T(8,128)} %fusion.26, bf16[12,64,4,128]{3,2,1,0:T(4,128)(2,1)S(1)} %reshape.233, f32[12,4,256,64]{2,3,1,0:T(8,128)} %copy-done.14, f32[12,4,64]{2,1,0:T(4,128)S(1)} %get-tuple-element.15), kind=kOutput, calls=%fused_computation.38 | convolution fusion | flops 209980672 | bytes 10235904 | tf_op jit(solution)/shard_map/chqk,cqhd->ckhd/dot_general | solution.py:45
  311.9 4.5 copy.64
  322.3 5.4 add_convert_fusion
  327.8 7.2 reshape.272
  335.0 4.9 broadcast_in_dim.54
  339.9 108.8 %scatter_fusion = bf16[48,114688]{1,0:T(8,128)(2,1)} fusion(bf16[48,114688]{1,0:T(8,128)(2,1)} %broadcast_in_dim.54, s32[24]{0:T(128)S(1)} %fusion.70, bf16[24,114688]{1,0:T(8,128)(2,1)} %reshape.272), kind=kCustom, calls=%fused_computation.3 | custom fusion | bytes 16515168 | tf_op jit(solution)/shard_map/scatter | solution.py:133
  448.7 17.2 %reshape.241 = bf16[16,3,114688]{2,1,0:T(4,128)(2,1)} reshape(bf16[48,114688]{1,0:T(8,128)(2,1)} %scatter_fusion) | data formatting | bytes 22020096 | tf_op jit(solution)/shard_map/reshape | solution.py:136
  465.9 5.0 all-to-all-start.2
  471.0 214.8 %all-to-all-done.2 = bf16[16,3,114688]{2,1,0:T(4,128)(2,1)} async-done(((bf16[16,3,114688]{2,1,0:T(4,128)(2,1)}), bf16[16,3,114688]{2,1,0:T(4,128)(2,1)}, u32[]{:S(2)}, u32[]{:S(2)}) %all-to-all-start.2) | async-done | bytes 11010080 | tf_op jit(solution)/shard_map/all_to_all | solution.py:135
  685.9 19.9 %reshape.242 = bf16[48,114688]{1,0:T(8,128)(2,1)} reshape(bf16[16,3,114688]{2,1,0:T(4,128)(2,1)} %all-to-all-done.2) | data formatting | bytes 22020096 | tf_op jit(solution)/shard_map/reshape | solution.py:142
  705.8 5.1 fusion.1
  710.8 5.2 copy.66
  722.0 4.3 fusion.12
  726.4 7.8 fusion.15
  734.2 4.0 fusion.47
  738.9 23.0 %fusion.50 = bf16[12,64,4,128]{3,1,2,0:T(8,128)(2,1)S(1)} fusion(bf16[12,256,4,128]{3,2,1,0:T(4,128)(2,1)} %reshape.232, f32[12,4,256,64]{2,3,1,0:T(8,128)} %fusion.26, f32[12,4,256,64]{2,3,1,0:T(8,128)} %copy-done.14, f32[12,4,64]{2,1,0:T(4,128)S(1)} %get-tuple-element.15), kind=kOutput, calls=%fused_computation.61 | convolution fusion | flops 208801024 | bytes 10235904 | tf_op jit(solution)/shard_map/chqk,ckhd->cqhd/dot_general | solution.py:42
  766.0 73.5 %reduce-scatter.12.cloned.1.call-done = f32[56,512]{1,0:T(8,128)} async-done(((f32[896,512]{1,0:T(8,128)}), f32[56,512]{1,0:T(8,128)}) %reduce-scatter.12.cloned.1.call-update) | async-done | bytes 114704
  839.4 76.9 %reduce-scatter.10.cloned.1.call-done = f32[56,512]{1,0:T(8,128)} async-done(((f32[896,512]{1,0:T(8,128)}), f32[56,512]{1,0:T(8,128)}) %reduce-scatter.10.cloned.1.call-update) | async-done | bytes 114704
  (78 shorter events, 29.1 us)
Async XLA Ops:
  7.2 248.4 %copy-start = (bf16[896,512]{1,0:T(8,128)(2,1)S(1)}, bf16[896,512]{1,0:T(8,128)(2,1)}, u32[]{:S(2)}) copy-start(bf16[896,512]{1,0:T(8,128)(2,1)} %param.14) | copy-start | bytes 2752516
  7.2 46.0 %all-gather.2.cloned.1.call-start = ((), (), s32[]{:S(2)}) async-start(), calls=%async_computation.6 | async-start | bytes 4128768 | tf_op jit(solution)/shard_map/all_gather | solution.py:55
  9.7 9.6 %copy-start.10 = (s32[12,2]{0,1:T(2,128)S(1)}, s32[12,2]{0,1:T(2,128)}, u32[]{:S(2)}) copy-start(s32[12,2]{0,1:T(2,128)} %param.16) | copy-start | bytes 292
  9.7 9.8 %copy-start.11 = (s32[12,2]{0,1:T(2,128)S(1)}, s32[12,2]{0,1:T(2,128)}, u32[]{:S(2)}) copy-start(s32[12,2]{0,1:T(2,128)} %param.17) | copy-start | bytes 292
  72.4 7.2 copy-start.8
  72.4 7.4 copy-start.9
  72.4 171.5 %all-to-all-start.1 = ((bf16[16,3,128,896]{3,2,1,0:T(8,128)(2,1)}), bf16[16,3,128,896]{3,2,1,0:T(8,128)(2,1)}, u32[]{:S(2)}, u32[]{:S(2)}) async-start(bf16[16,3,128,896]{3,2,1,0:T(8,128)(2,1)} %broadcast_select_fusion), calls=%async_computation.1 | async-start | bytes 22020096 | tf_op jit(solution)/shard_map/all_to_all | solution.py:100
  255.6 4.8 copy-start.12
  276.1 4.9 copy-start.3
  282.4 1.8 copy-start.14
  311.9 4.5 copy-start.7
  316.4 6.0 copy-start.5
  318.8 3.5 copy-start.4
  318.8 3.5 copy-start.13
  465.9 220.0 %all-to-all-start.2 = ((bf16[16,3,114688]{2,1,0:T(4,128)(2,1)}), bf16[16,3,114688]{2,1,0:T(4,128)(2,1)}, u32[]{:S(2)}, u32[]{:S(2)}) async-start(bf16[16,3,114688]{2,1,0:T(4,128)(2,1)} %reshape.241), calls=%async_computation.2 | async-start | bytes 29360128 | tf_op jit(solution)/shard_map/all_to_all | solution.py:135
  470.9 293.0 %reduce-scatter.8.cloned.1.call-start = ((), (), s32[]{:S(2)}) async-start(), calls=%async_computation.7 | async-start | bytes 8257536 | tf_op jit(solution)/shard_map/reduce_scatter | solution.py:64
  716.1 123.4 %reduce-scatter.12.cloned.1.call-start = ((), (), s32[]{:S(2)}) async-start(), calls=%async_computation.9 | async-start | bytes 1949696
  716.3 5.7 copy-start.6
  719.7 2.4 copy-start.2
  726.3 190.1 %reduce-scatter.10.cloned.1.call-start = ((), (), s32[]{:S(2)}) async-start(), calls=%async_computation.8 | async-start | bytes 1949696
  738.9 177.5 %copy-start.1 = (bf16[896,512]{1,0:T(8,128)(2,1)S(1)}, bf16[896,512]{1,0:T(8,128)(2,1)}, u32[]{:S(2)}) copy-start(bf16[896,512]{1,0:T(8,128)(2,1)} %param.14) | copy-start | bytes 2752516
Sparse Core Ops, SparseCore 0:
  19.3 33.7 all-gather.1
  716.2 46.9 reduce-scatter.7
  767.0 72.4 reduce-scatter.11
  843.1 73.2 reduce-scatter.9
where the time goes:
time: 930 us; the launch traced here: 923 us
  waiting for transfers between devices  546 us (59%)
  local copies, waits for them, and re-layouts  208 us (22%)
  matrix products  106 us (11%)
  other arithmetic  22.4 us (2%)
  between operations  14.3 us (2%)
  blocking collectives  13.8 us (1%)
  starting transfers between devices  12.6 us (1%)
    all_to_all x1, waiting for transfers between devices, body(): lax.all_to_all(placed.reshape(groups, capacity, row_len * feat_width), 's...  215 us
    all_to_all x1, waiting for transfers between devices, body(): lax.all_to_all(source_rows.reshape(groups, capacity, row_len, feat_width)...  164 us
    unnamed x6, waiting for transfers between devices  150 us
    scatter x1, local copies, waits for them, and re-layouts, body(): placed = jnp.zeros((slot_total, row_len * feat_width), jnp.bfloat16).at[p...  109 us
    dot_general x1, matrix products, attend(): jnp.einsum('chqk,cqhd->ckhd', mixed, queries, preferred_element_type=jnp....  24.5 us
    dot_general x1, matrix products, attend(): jnp.einsum('chqk,ckhd->cqhd', mixed, key_req, preferred_element_type=jnp....  23 us
    reshape x1, local copies, waits for them, and re-layouts, body(): returned = returned.reshape(slot_total, -1)  19.9 us
  transfers between devices with their start and end apart: 6, of which 5 were waited for; matrix products, arithmetic and copies ran while one was open for 5% of the time, Pallas kernels for 0%

commit v1 on v0

v1 whole, which is shorter than its diff:
```python
import functools
import math

import jax
import jax.numpy as jnp
from jax import lax
from jax.experimental import pallas as pl
from jax.experimental.pallas import tpu as pltpu
from jax.sharding import PartitionSpec as P

HD = 128
CAP = 3
MESH = pl.DeviceIdType.MESH
SIDE = 4
GROUPS = 16
RETS = 8
PIECES = 6
MIB = 1024 * 1024


def encode(raw_block, up_weight, down_weight):
    amount, row_len, feat_width = raw_block.shape
    inputs = raw_block.reshape(-1, feat_width).astype(jnp.float32)
    normed = (inputs * lax.rsqrt(jnp.mean(inputs * inputs, axis=-1, keepdims=True) + 1e-06)).astype(
        jnp.bfloat16
    )
    hidden = jax.nn.gelu(jnp.dot(normed, up_weight, preferred_element_type=jnp.float32)).astype(
        jnp.bfloat16
    )
    output = inputs + jnp.dot(hidden, down_weight, preferred_element_type=jnp.float32)
    return output.astype(jnp.bfloat16).reshape(amount, row_len, feat_width)


def ahead(seq, d):
    y, x = seq // SIDE, seq % SIDE
    return ((y + d // SIDE) % SIDE) * SIDE + (x + d % SIDE) % SIDE


def behind(seq, d):
    y, x = seq // SIDE, seq % SIDE
    return ((y + SIDE - d // SIDE) % SIDE) * SIDE + (x + SIDE - d % SIDE) % SIDE


def loop(low, high, step):
    def run(i, carry):
        step(i)
        return carry

    lax.fori_loop(low, high, run, 0)


def greet(seq, ret):
    barrier = pltpu.get_barrier_semaphore()

    def to_seq(d):
        pl.semaphore_signal(barrier, inc=1, device_id=(ahead(seq, d), ret), device_id_type=MESH)

    def to_ret(d):
        pl.semaphore_signal(barrier, inc=1, device_id=(seq, (ret + d) % RETS), device_id_type=MESH)

    loop(1, GROUPS, to_seq)
    loop(1, RETS, to_ret)
    pl.semaphore_wait(barrier, GROUPS + RETS - 2)


def remote(src, dst, send, recv, to):
    return pltpu.make_async_remote_copy(
        src_ref=src,
        dst_ref=dst,
        send_sem=send,
        recv_sem=recv,
        device_id=to,
        device_id_type=MESH,
    )


def fetch_kernel(
    enc,
    wanted,
    position,
    picked,
    served,
    table,
    arrived,
    leaving,
    own,
    served_s,
    id_send,
    id_recv,
    tab_send,
    tab_recv,
    seq_send,
    seq_recv,
    up_send,
    down_send,
    up_recv,
    down_recv,
    far_send,
    far_recv,
    sib_send,
    sib_recv,
    local,
):
    seq, ret = lax.axis_index("seq"), lax.axis_index("ret")
    z, core = ret // 2, ret % 2
    greet(seq, ret)

    def id_copy(d, dest, slot):
        return remote(wanted.at[dest], served.at[slot], id_send.at[d], id_recv.at[d], (dest, ret))

    def tab_copy(d, dest, slot):
        return remote(
            enc.at[:, dest],
            table.at[pl.ds(2 * slot, 2)],
            tab_send.at[d],
            tab_recv.at[d],
            (seq, dest),
        )

    loop(1, GROUPS, lambda d: id_copy(d, ahead(seq, d), seq).start())
    loop(1, RETS, lambda d: tab_copy(d, (ret + d) % RETS, ret).start())
    served[seq] = wanted[seq]
    table[2 * ret] = enc[0, ret]
    table[2 * ret + 1] = enc[1, ret]
    loop(1, GROUPS, lambda d: id_copy(d, ahead(seq, d), behind(seq, d)).wait())
    to_scalar = pltpu.make_async_copy(served, served_s, local.at[0])
    to_scalar.start()
    to_scalar.wait()
    loop(1, RETS, lambda d: tab_copy(d, (ret + d) % RETS, (ret + RETS - d) % RETS).wait())

    def seq_copy(d, dest, slot):
        return remote(
            leaving.at[dest], arrived.at[slot], seq_send.at[d], seq_recv.at[d], (dest, ret)
        )

    def serve(d):
        dest = ahead(seq, d)
        for k in range(CAP):
            leaving[dest, k] = table[jnp.maximum(served_s[dest, 0, k], 0)]
        seq_copy(d, dest, seq).start()

    loop(1, GROUPS, serve)
    for k in range(CAP):
        arrived[seq, k] = table[jnp.maximum(served_s[seq, 0, k], 0)]
    loop(1, GROUPS, lambda d: seq_copy(d, ahead(seq, d), behind(seq, d)).wait())

    requests = own.shape[0]

    def compact(i):
        at = position[i]
        own[i] = arrived[at // CAP, at % CAP]

    loop(0, requests, compact)

    size = requests // PIECES
    half = PIECES // 2
    above, below, facing = (z + 1) % SIDE, (z + SIDE - 1) % SIDE, (z + 2) % SIDE
    sibling = (seq, 2 * z + 1 - core)

    def rows(p):
        return pl.ds(p * size, size)

    def own_up(p, held):
        return remote(
            own.at[rows(p)],
            picked.at[rows(p), 2 * held + core],
            up_send.at[p],
            up_recv.at[p],
            (seq, 2 * above + core),
        )

    def own_down(p, held):
        return remote(
            own.at[rows(p)],
            picked.at[rows(p), 2 * held + core],
            down_send.at[p],
            down_recv.at[p],
            (seq, 2 * below + core),
        )

    def relay(p, held, to):
        return remote(
            picked.at[rows(p), 2 * held + core],
            picked.at[rows(p), 2 * held + core],
            far_send.at[p],
            far_recv.at[p],
            (seq, 2 * to + core),
        )

    def across(p, o, held, side):
        return remote(
            picked.at[rows(p), 2 * held + side],
            picked.at[rows(p), 2 * held + side],
            sib_send.at[o, p],
            sib_recv.at[o, p],
            sibling,
        )

    def own_across(p, side):
        return remote(
            own.at[rows(p)],
            picked.at[rows(p), 2 * z + side],
            sib_send.at[0, p],
            sib_recv.at[0, p],
            sibling,
        )

    for p in range(half):
        own_up(p, z).start()
        own_down(p + half, z).start()
    for p in range(half):
        own_up(p + half, z).start()
        own_down(p, z).start()
    for p in range(PIECES):
        own_across(p, core).start()
    keep = pltpu.make_async_copy(own, picked.at[:, ret], local.at[1])
    keep.start()
    for p in range(half):
        own_up(p, below).wait_recv()
        relay(p, below, above).start()
        across(p, 1, below, core).start()
        own_down(p + half, above).wait_recv()
        relay(p + half, above, below).start()
        across(p + half, 2, above, core).start()
    for p in range(half):
        own_up(p + half, below).wait_recv()
        across(p + half, 1, below, core).start()
        own_down(p, above).wait_recv()
        across(p, 2, above, core).start()
    for p in range(half):
        relay(p, facing, above).wait_recv()
        across(p, 3, facing, core).start()
        relay(p + half, facing, below).wait_recv()
        across(p + half, 3, facing, core).start()
    keep.wait()
    for p in range(PIECES):
        own_up(p, z).wait_send()
        own_down(p, z).wait_send()
        relay(p, below if p < half else above, above if p < half else below).wait_send()
        own_across(p, 1 - core).wait()
        across(p, 1, below, 1 - core).wait()
        across(p, 2, above, 1 - core).wait()
        across(p, 3, facing, 1 - core).wait()


def fetch(enc, wanted, position):
    requests = position.shape[0]
    feat = enc.shape[-1]
    enc = enc.reshape(2, RETS, 16, feat)
    dma = pltpu.SemaphoreType.DMA
    return pl.pallas_call(
        fetch_kernel,
        out_shape=(
            jax.ShapeDtypeStruct((requests, RETS, 16, feat), jnp.bfloat16),
            jax.ShapeDtypeStruct(wanted.shape, jnp.int32),
        ),
        in_specs=[
            pl.BlockSpec(memory_space=pltpu.VMEM),
            pl.BlockSpec(memory_space=pltpu.VMEM),
            pl.BlockSpec(memory_space=pltpu.SMEM),
        ],
        out_specs=(pl.BlockSpec(memory_space=pl.ANY), pl.BlockSpec(memory_space=pltpu.VMEM)),
        scratch_shapes=[
            pltpu.VMEM((2 * RETS, 16, feat), jnp.bfloat16),
            pltpu.VMEM((GROUPS, CAP, 16, feat), jnp.bfloat16),
            pltpu.VMEM((GROUPS, CAP, 16, feat), jnp.bfloat16),
            pltpu.VMEM((requests, 16, feat), jnp.bfloat16),
            pltpu.SMEM(wanted.shape, jnp.int32),
            dma((GROUPS,)),
            dma((GROUPS,)),
            dma((RETS,)),
            dma((RETS,)),
            dma((GROUPS,)),
            dma((GROUPS,)),
            dma((PIECES,)),
            dma((PIECES,)),
            dma((PIECES,)),
            dma((PIECES,)),
            dma((PIECES,)),
            dma((PIECES,)),
            dma((4, PIECES)),
            dma((4, PIECES)),
            dma((2,)),
        ],
        compiler_params=pltpu.CompilerParams(
            collective_id=0, has_side_effects=True, vmem_limit_bytes=32 * MIB
        ),
        name="fetch",
    )(enc, wanted, position)


NT = (((1,), (1,)), ((), ()))
TN = (((0,), (0,)), ((), ()))


def dot(a, b, dims=(((1,), (0,)), ((), ()))):
    return lax.dot_general(a, b, dims, preferred_element_type=jnp.float32)


def attend_kernel(
    picked, wk, wv, q, go, ctx, gq, part, gw, keys, values, gkeys, gvalues, acc_k, acc_v
):
    step = pl.program_id(0)
    spans = q.shape[0] // 64
    heads = q.shape[1] // HD
    scale = 1.0 / math.sqrt(HD)
    rows = picked[...]
    keys[...] = dot(rows, wk[...]).astype(jnp.bfloat16)
    values[...] = dot(rows, wv[...]).astype(jnp.bfloat16)
    for c in range(spans):
        tok = slice(64 * c, 64 * c + 64)
        row = slice(256 * c, 256 * c + 256)
        for h in range(heads):
            col = slice(HD * h, HD * h + HD)
            qh, gh = q[tok, col], go[tok, col]
            kh, vh = keys[row, col], values[row, col]
            weights = jnp.exp(dot(qh, kh, NT) * scale)
            weights = weights / jnp.sum(weights, axis=-1, keepdims=True)
            probs = weights.astype(jnp.bfloat16)
            ctx[tok, col] = dot(probs, vh).astype(jnp.bfloat16)
            gp = dot(gh, vh, NT)
            mixed = (
                weights * (gp - jnp.sum(weights * gp, axis=-1, keepdims=True)) * scale
            ).astype(jnp.bfloat16)
            gq[tok, col] = dot(mixed, kh).astype(jnp.bfloat16)
            gkeys[row, col] = dot(mixed, qh, TN).astype(jnp.bfloat16)
            gvalues[row, col] = dot(probs, gh, TN).astype(jnp.bfloat16)
    part[...] = (dot(gkeys[...], wk[...], NT) + dot(gvalues[...], wv[...], NT)).astype(jnp.bfloat16)
    add_k = dot(rows, gkeys[...], TN)
    add_v = dot(rows, gvalues[...], TN)

    @pl.when(step == 0)
    def _():
        acc_k[...] = add_k
        acc_v[...] = add_v

    @pl.when(step > 0)
    def _():
        acc_k[...] += add_k
        acc_v[...] += add_v

    @pl.when(step == pl.num_programs(0) - 1)
    def _():
        size = acc_k.shape[0] // GROUPS
        for j in range(GROUPS):
            own = slice(size * j, size * j + size)
            gw[j] = jnp.concatenate([acc_k[own], acc_v[own]], axis=0).astype(jnp.bfloat16)


def attend(picked, wk, wv, q, go, together=2):
    feat, width = wk.shape
    span_count = q.shape[0] // 64
    steps = span_count // together
    rows, toks = 256 * together, 64 * together
    whole = lambda i: (0, 0)
    along = lambda i: (i, 0)
    return pl.pallas_call(
        attend_kernel,
        grid=(steps,),
        out_shape=(
            jax.ShapeDtypeStruct(q.shape, jnp.bfloat16),
            jax.ShapeDtypeStruct(q.shape, jnp.bfloat16),
            jax.ShapeDtypeStruct(picked.shape, jnp.bfloat16),
            jax.ShapeDtypeStruct((GROUPS, 2 * feat // GROUPS, width), jnp.bfloat16),
        ),
        in_specs=[
            pl.BlockSpec((rows, feat), along),
            pl.BlockSpec((feat, width), whole),
            pl.BlockSpec((feat, width), whole),
            pl.BlockSpec((toks, width), along),
            pl.BlockSpec((toks, width), along),
        ],
        out_specs=(
            pl.BlockSpec((toks, width), along),
            pl.BlockSpec((toks, width), along),
            pl.BlockSpec((rows, feat), along),
            pl.BlockSpec((GROUPS, 2 * feat // GROUPS, width), lambda i: (0, 0, 0)),
        ),
        scratch_shapes=[
            pltpu.VMEM((rows, width), jnp.bfloat16),
            pltpu.VMEM((rows, width), jnp.bfloat16),
            pltpu.VMEM((rows, width), jnp.bfloat16),
            pltpu.VMEM((rows, width), jnp.bfloat16),
            pltpu.VMEM((feat, width), jnp.float32),
            pltpu.VMEM((feat, width), jnp.float32),
        ],
        compiler_params=pltpu.CompilerParams(
            dimension_semantics=("arbitrary",), vmem_limit_bytes=48 * MIB
        ),
        name="attend",
    )(picked, wk, wv, q, go)


def give_kernel(
    part,
    gw,
    served,
    source,
    home,
    gk_out,
    gv_out,
    acc,
    sib,
    near_up,
    near_down,
    far,
    total,
    leaving,
    arrived,
    table,
    wsum,
    w_send,
    w_recv,
    own_sem,
    sib_send,
    sib_recv,
    up_send,
    up_recv,
    down_send,
    down_recv,
    far_send,
    far_recv,
    seq_send,
    seq_recv,
    tab_send,
    tab_recv,
    keep,
):
    seq, ret = lax.axis_index("seq"), lax.axis_index("ret")
    z, core = ret // 2, ret % 2
    requests = total.shape[0]
    size = requests // PIECES
    half = PIECES // 2
    above, below = (z + 1) % SIDE, (z + SIDE - 1) % SIDE
    greet(seq, ret)

    def own_copy(o):
        return pltpu.make_async_copy(part.at[:, (z + o) % SIDE, core], acc.at[o], own_sem.at[o])

    def sib_copy(o):
        return remote(
            part.at[:, (z + o) % SIDE, 1 - core],
            sib.at[o],
            sib_send.at[o],
            sib_recv.at[o],
            (seq, 2 * z + 1 - core),
        )

    def w_copy(d, dest):
        return remote(gw.at[dest], wsum.at[d], w_send.at[d], w_recv.at[d], (dest, ret))

    for o in (2, 1, 3, 0):
        own_copy(o).start()
        sib_copy(o).start()
    loop(1, GROUPS, lambda d: w_copy(d, ahead(seq, d)).start())
    own_w = pltpu.make_async_copy(gw.at[seq], wsum.at[0], w_send.at[0])
    own_w.start()

    def rows(p):
        return pl.ds(p * size, size)

    def merge(o):
        own_copy(o).wait()
        sib_copy(o).wait_recv()

        def one(i):
            acc[o, i] = (acc[o, i].astype(jnp.float32) + sib[o, i].astype(jnp.float32)).astype(
                jnp.bfloat16
            )

        loop(0, requests, one)

    def add_far(o, p):
        def one(i):
            acc[o, i] = (acc[o, i].astype(jnp.float32) + far[i].astype(jnp.float32)).astype(
                jnp.bfloat16
            )

        loop(p * size, p * size + size, one)

    up_to, down_to = (seq, 2 * above + core), (seq, 2 * below + core)

    def far_copy(p):
        return remote(
            acc.at[2, rows(p)],
            far.at[rows(p)],
            far_send.at[p],
            far_recv.at[p],
            up_to if p < half else down_to,
        )

    def up_copy(p):
        return remote(acc.at[1, rows(p)], near_up.at[rows(p)], up_send.at[p], up_recv.at[p], up_to)

    def down_copy(p):
        return remote(
            acc.at[3, rows(p)], near_down.at[rows(p)], down_send.at[p], down_recv.at[p], down_to
        )

    merge(2)
    for p in range(half):
        far_copy(p).start()
        far_copy(p + half).start()
    merge(1)
    for p in range(half):
        up_copy(p + half).start()
    merge(3)
    for p in range(half):
        down_copy(p).start()
    merge(0)
    for p in range(half):
        far_copy(p).wait_recv()
        add_far(1, p)
        up_copy(p).start()
        far_copy(p + half).wait_recv()
        add_far(3, p + half)
        down_copy(p + half).start()
    for p in range(half):
        up_copy(p + half).wait_recv()
        down_copy(p).wait_recv()
    for p in range(half):
        up_copy(p).wait_recv()
        down_copy(p + half).wait_recv()

    def finish(i):
        total[i] = (
            acc[0, i].astype(jnp.float32)
            + near_up[i].astype(jnp.float32)
            + near_down[i].astype(jnp.float32)
        ).astype(jnp.bfloat16)

    loop(0, requests, finish)

    def seq_copy(d, dest, slot):
        return remote(
            leaving.at[dest], arrived.at[slot], seq_send.at[d], seq_recv.at[d], (dest, ret)
        )

    def give_back(d):
        dest = ahead(seq, d)
        for k in range(CAP):
            leaving[dest, k] = total[source[dest * CAP + k]]
        seq_copy(d, dest, seq).start()

    loop(1, GROUPS, give_back)
    for k in range(CAP):
        arrived[seq, k] = total[source[seq * CAP + k]]

    own_w.wait()
    loop(1, GROUPS, lambda d: w_copy(d, ahead(seq, d)).wait())
    rows_w = gk_out.shape[0]
    for c in range(0, gk_out.shape[1], 128):
        col = pl.ds(c, 128)
        w_total = wsum[0, :, col].astype(jnp.float32)
        for d in range(1, GROUPS):
            w_total = w_total + wsum[d, :, col].astype(jnp.float32)
        gk_out[:, col] = w_total[:rows_w]
        gv_out[:, col] = w_total[rows_w:]

    loop(1, GROUPS, lambda d: seq_copy(d, ahead(seq, d), behind(seq, d)).wait())

    def tab_copy(d, dest, slot):
        return remote(
            table.at[pl.ds(2 * dest, 2)],
            home.at[:, slot],
            tab_send.at[d],
            tab_recv.at[d],
            (seq, dest),
        )

    feat = total.shape[-1]

    def sum_slot(slot):
        def add(s, carry):
            for k in range(CAP):
                here = served[s, 0, k] == slot
                carry = carry + jnp.where(here, arrived[s, k].astype(jnp.float32), 0.0)
            return carry

        table[slot] = lax.fori_loop(0, GROUPS, add, jnp.zeros((16, feat), jnp.float32)).astype(
            jnp.bfloat16
        )

    def send_home(d):
        dest = (ret + d) % RETS
        sum_slot(2 * dest)
        sum_slot(2 * dest + 1)
        tab_copy(d, dest, ret).start()

    loop(1, RETS, send_home)
    sum_slot(2 * ret)
    sum_slot(2 * ret + 1)
    kept = pltpu.make_async_copy(table.at[pl.ds(2 * ret, 2)], home.at[:, ret], keep)
    kept.start()
    kept.wait()
    loop(1, RETS, lambda d: tab_copy(d, (ret + d) % RETS, (ret + RETS - d) % RETS).wait())
    for o in range(4):
        sib_copy(o).wait_send()
    for p in range(PIECES):
        far_copy(p).wait_send()
        up_copy(p).wait_send()
        down_copy(p).wait_send()


def give(part, gw, served, source):
    requests, feat = part.shape[0] // 128, part.shape[1]
    part = part.reshape(requests, SIDE, 2, 16, feat)
    _, rows_w, width = gw.shape
    dma = pltpu.SemaphoreType.DMA
    chunk = (requests, 16, feat)
    vmem = pl.BlockSpec(memory_space=pltpu.VMEM)
    home, gk, gv = pl.pallas_call(
        give_kernel,
        out_shape=(
            jax.ShapeDtypeStruct((2, RETS, 16, feat), jnp.bfloat16),
            jax.ShapeDtypeStruct((rows_w // 2, width), jnp.float32),
            jax.ShapeDtypeStruct((rows_w // 2, width), jnp.float32),
        ),
        in_specs=[
            pl.BlockSpec(memory_space=pl.ANY),
            pl.BlockSpec(memory_space=pl.ANY),
            pl.BlockSpec(memory_space=pltpu.SMEM),
            pl.BlockSpec(memory_space=pltpu.SMEM),
        ],
        out_specs=(vmem, vmem, vmem),
        scratch_shapes=[
            pltpu.VMEM((4,) + chunk, jnp.bfloat16),
            pltpu.VMEM((4,) + chunk, jnp.bfloat16),
            pltpu.VMEM(chunk, jnp.bfloat16),
            pltpu.VMEM(chunk, jnp.bfloat16),
            pltpu.VMEM(chunk, jnp.bfloat16),
            pltpu.VMEM(chunk, jnp.bfloat16),
            pltpu.VMEM((GROUPS, CAP, 16, feat), jnp.bfloat16),
            pltpu.VMEM((GROUPS, CAP, 16, feat), jnp.bfloat16),
            pltpu.VMEM((2 * RETS, 16, feat), jnp.bfloat16),
            pltpu.VMEM(gw.shape, jnp.bfloat16),
            dma((GROUPS,)),
            dma((GROUPS,)),
            dma((4,)),
            dma((4,)),
            dma((4,)),
            dma((PIECES,)),
            dma((PIECES,)),
            dma((PIECES,)),
            dma((PIECES,)),
            dma((PIECES,)),
            dma((PIECES,)),
            dma((GROUPS,)),
            dma((GROUPS,)),
            dma((RETS,)),
            dma((RETS,)),
            dma,
        ],
        compiler_params=pltpu.CompilerParams(
            collective_id=1, has_side_effects=True, vmem_limit_bytes=32 * MIB
        ),
        name="give",
    )(part, gw, served, source)
    return home.reshape(2, 128, feat), gk, gv


def body(
    queries,
    grad_ctx,
    neighbours,
    up_weight,
    down_weight,
    key_weight,
    value_weight,
    group_ids,
    slot_ids,
):
    targets, slots = group_ids.reshape(-1), slot_ids.reshape(-1)
    requests = targets.shape[0]
    order = jnp.arange(requests, dtype=jnp.int32)
    earlier = (targets[:, None] == targets[None, :]) & (order[None, :] < order[:, None])
    position = targets * CAP + jnp.sum(earlier.astype(jnp.int32), axis=1)
    match = position[:, None] == jnp.arange(GROUPS * CAP, dtype=jnp.int32)[None, :]
    wanted = jnp.sum(jnp.where(match, slots[:, None] + 1, 0), axis=0) - 1
    source = jnp.sum(jnp.where(match, order[:, None], 0), axis=0)
    wanted = jnp.pad(wanted.reshape(GROUPS, 1, CAP), ((0, 0), (0, 7), (0, 128 - CAP)))

    encoded = encode(neighbours, up_weight, down_weight)
    picked, served = fetch(encoded, wanted, position)
    feat = picked.shape[-1]
    context, grad_query, part, gw = attend(
        picked.reshape(-1, feat), key_weight, value_weight, queries, grad_ctx
    )
    grad_encoded, grad_key_w, grad_value_w = give(part, gw, served, source)
    return context, grad_query, grad_encoded, grad_key_w, grad_value_w


def solution(mesh):
    return jax.shard_map(
        body,
        mesh=mesh,
        in_specs=(
            P("seq", "ret"),
            P("seq", "ret"),
            P(("seq", "ret"), None, None),
            P(),
            P(),
            P(None, "ret"),
            P(None, "ret"),
            P("seq", None),
            P("seq", None),
        ),
        out_specs=(
            P("seq", "ret"),
            P("seq", "ret"),
            P(("seq", "ret"), None, None),
            P("seq", "ret"),
            P("seq", "ret"),
        ),
        check_vma=False,
    )
```

time: 930 us -> 195 us (0.21)
  waiting for transfers between devices: 546 us -> 0 us
  local copies, waits for them, and re-layouts: 208 us -> 9.16 us
  Pallas kernels: 0 us -> 171 us
  matrix products: 106 us -> 9.77 us
  other arithmetic: 22.4 us -> 4.1 us
  blocking collectives: 13.8 us -> 0 us
  between operations: 14.3 us -> 0.7 us
  starting transfers between devices: 12.6 us -> 0 us
    all_to_all x2 -> x0, waiting for transfers between devices: 379 us -> none  [the longest x1 215 us: body(): lax.all_to_all(placed.reshape(groups, capacity, row_len * feat_width), 's...]
    pallas_call x0 -> x3, Pallas kernels: none -> 171 us  [the longest x1 64.4 us: give(): pl.pallas_call(give_kernel, out_shape=(jax.ShapeDtypeStruct((2, RETS, 16,...]
    unnamed x6 -> x0, waiting for transfers between devices: 150 us -> none
    scatter x2 -> x0, local copies, waits for them, and re-layouts: 109 us -> none  [the longest x1 109 us: body(): placed = jnp.zeros((slot_total, row_len * feat_width), jnp.bfloat16).at[p...]
    dot_general x13 -> x0, matrix products: 96.5 us -> none  [the longest x1 24.5 us: attend(): jnp.einsum('chqk,cqhd->ckhd', mixed, queries, preferred_element_type=jnp....]
    reshape x12 -> x1, local copies, waits for them, and re-layouts: 57.4 us -> 0.08 us  [body(): targets, slots = (group_ids.reshape(-1), slot_ids.reshape(-1))]
    gather x2 -> x0, local copies, waits for them, and re-layouts: 17.3 us -> none  [the longest x1 9.26 us: body(): source_rows = jnp.take(enc_table, served, axis=0)]
    all_gather x1 -> x0, waiting for transfers between devices: 17 us -> none  [full_table(): return lax.all_gather(encoded_own, 'ret', axis=0, tiled=True)]
  transfers between devices with their start and end apart: 6 -> 0, of which waited for: 5 -> 0; matrix products, arithmetic and copies ran while one was open for 5% -> 0% of each run, Pallas kernels for 0% -> 0%
where the time goes in v1:
time: 195 us; the launch traced here: 194 us
  Pallas kernels  171 us (88%)
  matrix products  9.77 us (5%)
  local copies, waits for them, and re-layouts  9.16 us (5%)
  other arithmetic  4.1 us (2%)
    pallas_call x1, Pallas kernels, give(): pl.pallas_call(give_kernel, out_shape=(jax.ShapeDtypeStruct((2, RETS, 16,...  64.4 us
    pallas_call x1, Pallas kernels, fetch(): pl.pallas_call(fetch_kernel, out_shape=(jax.ShapeDtypeStruct((requests, R...  62.8 us
    pallas_call x1, Pallas kernels, attend(): pl.pallas_call(attend_kernel, grid=(steps,), out_shape=(jax.ShapeDtypeStr...  43.6 us
    dot_general x1, matrix products, encode(): jnp.dot(hidden, down_weight, preferred_element_type=jnp.float32)  9.77 us
    unnamed x18, local copies, waits for them, and re-layouts  8.8 us

profile of v1, /device:TPU:1, one launch (start us, length us, event | category | flops | bytes accessed | tf_op | source)
XLA Modules:
  0.0 194.4 jit_solution(16055438624925283815)
XLA Ops:
  0.6 0.7 broadcast_add_fusion
  1.3 1.2 multiply_reduce_fusion
  2.5 0.1 copy.21
  2.6 0.1 add.57
  2.7 0.8 copy.20
  3.5 0.1 reshape.74
  3.6 0.2 convert_reduce_fusion
  3.7 0.1 select_reduce_fusion
  3.8 0.1 sub.7
  4.0 1.9 fusion.20
  5.9 0.0 copy-start.2
  5.9 0.0 copy-start.3
  5.9 0.0 copy-start.4
  5.9 0.0 copy-start.5
  5.9 9.8 %fusion.17 = bf16[256,896]{1,0:T(8,128)(2,1)} fusion(bf16[3584,896]{1,0:T(8,128)(2,1)} %param.13, bf16[256,896]{1,0:T(8,128)(2,1)} %fusion.20, bf16[896,3584]{1,0:T(8,128)(2,1)} %param.12, bf16[256,896]{1,0:T(8,128)(2,1)} %bitcast.19), kind=kOutput, calls=%fused_computation.15 | convolution fusion | flops 3297280000 | bytes 14221312 | tf_op jit(solution)/shard_map/dot_general | solution.py:30
  15.7 0.0 copy-start.6
  15.7 1.0 copy-done.6
  16.7 62.8 %fetch.1 = (bf16[24,8,16,896]{3,2,1,0:T(8,128)(2,1)S(1)}, s32[16,8,128]{2,1,0:T(8,128)S(1)}) custom-call(bf16[2,8,16,896]{3,2,1,0:T(8,128)(2,1)S(1)} %bitcast.18, s32[16,8,128]{2,1,0:T(8,128)S(1)} %pad.4.wanted, s32[24]{0:T(128)S(1)} %multiply_add_fusion.position), custom_call_target="tpu_custom_call" | custom-call | tf_op jit(solution)/shard_map/fetch/pallas_call | solution.py:251
  79.5 0.0 copy-start
  79.5 2.4 %copy-done = bf16[24,8,16,896]{3,2,1,0:T(8,128)(2,1)} copy-done((bf16[24,8,16,896]{3,2,1,0:T(8,128)(2,1)}, bf16[24,8,16,896]{3,2,1,0:T(8,128)(2,1)S(1)}, u32[]{:S(2)}) %copy-start) | copy-done | bytes 5505048
  81.8 0.0 copy-done.2
  81.8 0.0 copy-done.3
  81.8 0.0 copy-done.4
  81.8 0.0 copy-done.5
  81.9 43.6 %attend.1 = (bf16[768,512]{1,0:T(8,128)(2,1)}, bf16[768,512]{1,0:T(8,128)(2,1)}, bf16[3072,896]{1,0:T(8,128)(2,1)}, bf16[16,112,512]{2,1,0:T(8,128)(2,1)S(1)}) custom-call(bf16[3072,896]{1,0:T(8,128)(2,1)} %bitcast.15, bf16[896,512]{1,0:T(8,128)(2,1)S(1)} %copy-done.2, bf16[896,512]{1,0:T(8,128)(2,1)S(1)} %copy-done.3, bf16[768,512]{1,0:T(8,128)(2,1)S(1)} %copy-done.4, ...), custom_call_target="tpu_custom_call" | custom-call | tf_op jit(solution)/shard_map/attend/pallas_call | solution.py:357
  125.4 0.0 copy-start.1
  125.4 2.6 %copy-done.1 = bf16[3072,896]{1,0:T(8,128)(2,1)S(1)} copy-done((bf16[3072,896]{1,0:T(8,128)(2,1)S(1)}, bf16[3072,896]{1,0:T(8,128)(2,1)}, u32[]{:S(2)}) %copy-start.1) | copy-done | bytes 5505048
  128.0 64.4 %give.1 = (bf16[2,8,16,896]{3,2,1,0:T(8,128)(2,1)S(1)}, f32[56,512]{1,0:T(8,128)S(1)}, f32[56,512]{1,0:T(8,128)S(1)}) custom-call(bf16[24,4,2,16,896]{4,3,2,1,0:T(8,128)(2,1)S(1)} %bitcast.16, bf16[16,112,512]{2,1,0:T(8,128)(2,1)S(1)} %get-tuple-element.18.gw, s32[16,8,128]{2,1,0:T(8,128)S(1)} %get-tuple-element.19.served, s32[48]{0:T(128)S(1)} %get-tuple-element.23.source), custom_call_target="tpu_custom_call" | custom-call | tf_op jit(solution)/shard_map/give/pallas_call | solution.py:612
  192.3 0.8 copy.26
  193.1 0.6 copy.27
  193.8 0.6 copy.28
  (4 shorter events, 0.0 us)
Async XLA Ops:
  5.9 76.0 %copy-start.2 = (bf16[896,512]{1,0:T(8,128)(2,1)S(1)}, bf16[896,512]{1,0:T(8,128)(2,1)}, u32[]{:S(2)}) copy-start(bf16[896,512]{1,0:T(8,128)(2,1)} %wk.1) | copy-start | bytes 2752516
  5.9 76.0 %copy-start.3 = (bf16[896,512]{1,0:T(8,128)(2,1)S(1)}, bf16[896,512]{1,0:T(8,128)(2,1)}, u32[]{:S(2)}) copy-start(bf16[896,512]{1,0:T(8,128)(2,1)} %wv.1) | copy-start | bytes 2752516
  5.9 76.0 %copy-start.4 = (bf16[768,512]{1,0:T(8,128)(2,1)S(1)}, bf16[768,512]{1,0:T(8,128)(2,1)}, u32[]{:S(2)}) copy-start(bf16[768,512]{1,0:T(8,128)(2,1)} %q.1) | copy-start | bytes 2359300
  5.9 76.0 %copy-start.5 = (bf16[768,512]{1,0:T(8,128)(2,1)S(1)}, bf16[768,512]{1,0:T(8,128)(2,1)}, u32[]{:S(2)}) copy-start(bf16[768,512]{1,0:T(8,128)(2,1)} %go.1) | copy-start | bytes 2359300
  15.7 1.0 copy-start.6
  79.5 2.4 %copy-start = (bf16[24,8,16,896]{3,2,1,0:T(8,128)(2,1)}, bf16[24,8,16,896]{3,2,1,0:T(8,128)(2,1)S(1)}, u32[]{:S(2)}) copy-start(bf16[24,8,16,896]{3,2,1,0:T(8,128)(2,1)S(1)} %get-tuple-element.14) | copy-start | bytes 16515076
  125.4 2.6 %copy-start.1 = (bf16[3072,896]{1,0:T(8,128)(2,1)S(1)}, bf16[3072,896]{1,0:T(8,128)(2,1)}, u32[]{:S(2)}) copy-start(bf16[3072,896]{1,0:T(8,128)(2,1)} %get-tuple-element.17) | copy-start | bytes 16515076

commit v2 on v0

v2 whole, which is shorter than its diff:
```python
import functools
import math

import jax
import jax.numpy as jnp
from jax import lax
from jax.experimental import pallas as pl
from jax.experimental.pallas import tpu as pltpu
from jax.sharding import PartitionSpec as P

HD = 128
CAP = 3
MESH = pl.DeviceIdType.MESH
SIDE = 4
GROUPS = 16
RETS = 8
STEPS = 6
BLOCKS = 7
EARLY = 2
MIB = 1024 * 1024


def ahead(seq, d):
    y, x = seq // SIDE, seq % SIDE
    return ((y + d // SIDE) % SIDE) * SIDE + (x + d % SIDE) % SIDE


def behind(seq, d):
    y, x = seq // SIDE, seq % SIDE
    return ((y + SIDE - d // SIDE) % SIDE) * SIDE + (x + SIDE - d % SIDE) % SIDE


def loop(low, high, step):
    def run(i, carry):
        step(i)
        return carry

    lax.fori_loop(low, high, run, 0)


def greet(seq, ret):
    barrier = pltpu.get_barrier_semaphore()

    def to_seq(d):
        pl.semaphore_signal(barrier, inc=1, device_id=(ahead(seq, d), ret), device_id_type=MESH)

    def to_ret(d):
        pl.semaphore_signal(barrier, inc=1, device_id=(seq, (ret + d) % RETS), device_id_type=MESH)

    loop(1, GROUPS, to_seq)
    loop(1, RETS, to_ret)
    pl.semaphore_wait(barrier, GROUPS + RETS - 2)


def remote(src, dst, send, recv, to):
    return pltpu.make_async_remote_copy(
        src_ref=src,
        dst_ref=dst,
        send_sem=send,
        recv_sem=recv,
        device_id=to,
        device_id_type=MESH,
    )


NT = (((1,), (1,)), ((), ()))
TN = (((0,), (0,)), ((), ()))


def dot(a, b, dims=(((1,), (0,)), ((), ()))):
    return lax.dot_general(a, b, dims, preferred_element_type=jnp.float32)


class Refs:
    def __init__(self, names, refs):
        self.__dict__.update(zip(names, refs))


def kernel(names, *refs):
    r = Refs(names, refs)
    seq, ret = lax.axis_index("seq"), lax.axis_index("ret")
    z, core = ret // 2, ret % 2
    above, below, facing = (z + 1) % SIDE, (z + SIDE - 1) % SIDE, (z + 2) % SIDE
    sibling = (seq, 2 * z + 1 - core)
    up_to, down_to = (seq, 2 * above + core), (seq, 2 * below + core)
    requests = r.own.shape[0]
    size = requests // STEPS
    half = size // 2
    feat = r.own.shape[-1]

    def up_load(j):
        width = r.up_w.shape[-1]
        return pltpu.make_async_copy(
            r.up_weight.at[:, pl.ds(j * width, width)], r.up_w.at[j], r.up_sem.at[j]
        )

    def down_load(j):
        depth = r.down_w.shape[1]
        return pltpu.make_async_copy(
            r.down_weight.at[pl.ds(j * depth, depth)], r.down_w.at[j], r.down_sem.at[j]
        )

    loads = [
        pltpu.make_async_copy(a, b, r.load_sem.at[i])
        for i, (a, b) in enumerate(
            (
                (r.key_weight, r.wk),
                (r.value_weight, r.wv),
                (r.queries, r.q),
                (r.grad_ctx, r.go),
                (r.neighbours.at[:, ret], r.raw.at[pl.ds(2 * ret, 2)]),
            )
        )
    ]
    loads[4].start()
    for j in range(BLOCKS):
        up_load(j).start()
        down_load(j).start()
    for i in range(4):
        loads[i].start()

    greet(seq, ret)

    def id_copy(d, dest, slot):
        return remote(
            r.wanted.at[dest], r.served.at[slot], r.id_send.at[d], r.id_recv.at[d], (dest, ret)
        )

    def raw_copy(d, dest, slot):
        return remote(
            r.neighbours.at[:, dest],
            r.raw.at[pl.ds(2 * slot, 2)],
            r.raw_send.at[d],
            r.raw_recv.at[d],
            (seq, dest),
        )

    loop(1, RETS, lambda d: raw_copy(d, (ret + d) % RETS, ret).start())
    loop(1, GROUPS, lambda d: id_copy(d, ahead(seq, d), seq).start())
    r.served[seq] = r.wanted[seq]
    loads[4].wait()
    loop(1, RETS, lambda d: raw_copy(d, (ret + d) % RETS, (ret + RETS - d) % RETS).wait())

    inputs = r.raw[...].reshape(-1, feat).astype(jnp.float32)
    normed = inputs * lax.rsqrt(jnp.mean(inputs * inputs, axis=-1, keepdims=True) + 1e-06)
    r.normed[...] = normed.astype(jnp.bfloat16)
    r.encoding[...] = inputs

    def feed(j):
        up_load(j).wait()
        hidden = jax.nn.gelu(dot(r.normed[...], r.up_w[j])).astype(jnp.bfloat16)
        down_load(j).wait()
        r.encoding[...] += dot(hidden, r.down_w[j])

    loop(0, BLOCKS, feed)
    r.table[...] = r.encoding[...].astype(jnp.bfloat16).reshape(r.table.shape)

    loop(1, GROUPS, lambda d: id_copy(d, ahead(seq, d), behind(seq, d)).wait())
    to_scalar = pltpu.make_async_copy(r.served, r.served_s, r.scalar_sem)
    to_scalar.start()
    to_scalar.wait()

    def seq_copy(d, dest, slot):
        return remote(
            r.leaving.at[dest], r.arrived.at[slot], r.seq_send.at[d], r.seq_recv.at[d], (dest, ret)
        )

    def serve(d):
        dest = ahead(seq, d)
        for k in range(CAP):
            r.leaving[dest, k] = r.table[jnp.maximum(r.served_s[dest, 0, k], 0)]
        seq_copy(d, dest, seq).start()

    loop(1, GROUPS, serve)
    for k in range(CAP):
        r.arrived[seq, k] = r.table[jnp.maximum(r.served_s[seq, 0, k], 0)]
    loop(1, GROUPS, lambda d: seq_copy(d, ahead(seq, d), behind(seq, d)).wait())

    def compact(i):
        at = r.position[i]
        r.own[i] = r.arrived[at // CAP, at % CAP]

    loop(0, requests, compact)
    for i in range(4):
        loads[i].wait()

    def rows(g, h):
        return pl.ds(g * size + h * half, half)

    def own_up(g, h, held):
        return remote(
            r.own.at[rows(g, h)],
            r.picked.at[rows(g, h), 2 * held + core],
            r.up_send.at[g, h],
            r.up_recv.at[g, h],
            up_to,
        )

    def own_down(g, h, held):
        return remote(
            r.own.at[rows(g, h)],
            r.picked.at[rows(g, h), 2 * held + core],
            r.dn_send.at[g, h],
            r.dn_recv.at[g, h],
            down_to,
        )

    def relay(g, h, held):
        return remote(
            r.picked.at[rows(g, h), 2 * held + core],
            r.picked.at[rows(g, h), 2 * held + core],
            r.far_send.at[g, h],
            r.far_recv.at[g, h],
            down_to if h else up_to,
        )

    def across(g, o, held, side):
        whole = pl.ds(g * size, size)
        source = r.picked.at[whole, 2 * held + side]
        return remote(
            r.own.at[whole] if o == 0 else source,
            source,
            r.sib_send.at[g, o],
            r.sib_recv.at[g, o],
            sibling,
        )

    def keep(g):
        whole = pl.ds(g * size, size)
        return pltpu.make_async_copy(
            r.own.at[whole], r.picked.at[whole, ret], r.keep_sem.at[g]
        )

    def send_own(g):
        own_up(g, 0, z).start()
        own_down(g, 1, z).start()
        own_up(g, 1, z).start()
        own_down(g, 0, z).start()
        across(g, 0, z, core).start()
        keep(g).start()

    def pass_on(g):
        own_up(g, 0, below).wait_recv()
        relay(g, 0, below).start()
        own_down(g, 1, above).wait_recv()
        relay(g, 1, above).start()
        own_up(g, 1, below).wait_recv()
        across(g, 1, below, core).start()
        own_down(g, 0, above).wait_recv()
        across(g, 2, above, core).start()

    def pass_far(g):
        relay(g, 0, facing).wait_recv()
        relay(g, 1, facing).wait_recv()
        across(g, 3, facing, core).start()

    def settle(g):
        for h in range(2):
            own_up(g, h, z).wait_send()
            own_down(g, h, z).wait_send()
            relay(g, h, above if h else below).wait_send()
        keep(g).wait()
        across(g, 0, z, 1 - core).wait()
        across(g, 1, below, 1 - core).wait()
        across(g, 2, above, 1 - core).wait()
        across(g, 3, facing, 1 - core).wait()

    def swap(g, o):
        whole = pl.ds(g * size, size)
        return remote(
            r.part.at[whole, (z + o) % SIDE, 1 - core],
            r.sib.at[o, whole],
            r.swap_send.at[g, o],
            r.swap_recv.at[g, o],
            sibling,
        )

    def far_copy(g, h):
        return remote(
            r.part.at[rows(g, h), facing, core],
            r.far.at[rows(g, h)],
            r.rfar_send.at[g, h],
            r.rfar_recv.at[g, h],
            down_to if h else up_to,
        )

    def up_copy(g, h):
        return remote(
            r.part.at[rows(g, h), above, core],
            r.near_up.at[rows(g, h)],
            r.rup_send.at[g, h],
            r.rup_recv.at[g, h],
            up_to,
        )

    def down_copy(g, h):
        return remote(
            r.part.at[rows(g, h), below, core],
            r.near_down.at[rows(g, h)],
            r.rdn_send.at[g, h],
            r.rdn_recv.at[g, h],
            down_to,
        )

    def merge(g, o):
        swap(g, o).wait_recv()
        at = (z + o) % SIDE

        def one(i):
            r.part[i, at, core] = (
                r.part[i, at, core].astype(jnp.float32) + r.sib[o, i].astype(jnp.float32)
            ).astype(jnp.bfloat16)

        loop(g * size, g * size + size, one)

    def merge_all(g):
        merge(g, 2)
        far_copy(g, 0).start()
        far_copy(g, 1).start()
        merge(g, 1)
        up_copy(g, 1).start()
        merge(g, 3)
        down_copy(g, 0).start()
        merge(g, 0)

    def add_far(g, h):
        far_copy(g, h).wait_recv()
        at = below if h else above

        def one(i):
            r.part[i, at, core] = (
                r.part[i, at, core].astype(jnp.float32) + r.far[i].astype(jnp.float32)
            ).astype(jnp.bfloat16)

        loop(g * size + h * half, g * size + h * half + half, one)
        (down_copy if h else up_copy)(g, h).start()

    def finish(g):
        for h in range(2):
            up_copy(g, h).wait_recv()
            down_copy(g, h).wait_recv()

        def one(i):
            r.total[i] = (
                r.part[i, z, core].astype(jnp.float32)
                + r.near_up[i].astype(jnp.float32)
                + r.near_down[i].astype(jnp.float32)
            ).astype(jnp.bfloat16)

        loop(g * size, g * size + size, one)
        for o in range(4):
            swap(g, o).wait_send()
        for h in range(2):
            far_copy(g, h).wait_send()
            up_copy(g, h).wait_send()
            down_copy(g, h).wait_send()

    def result_copies(g):
        tokens = pl.ds(g * (size * 32), size * 32)
        return (
            pltpu.make_async_copy(r.ctx.at[tokens], r.context.at[tokens], r.out_sem.at[g, 0]),
            pltpu.make_async_copy(r.gq.at[tokens], r.grad_query.at[tokens], r.out_sem.at[g, 1]),
        )

    def compute(g):
        attend(r, g, size)
        for o in (2, 1, 3, 0):
            swap(g, o).start()
        for copy in result_copies(g):
            copy.start()

    def at_step(g, step):
        @pl.when((g >= 0) & (g < STEPS))
        def _():
            step(g)

    for g in range(EARLY):
        send_own(g)

    def tick(t):
        at_step(t + EARLY, send_own)
        at_step(t, pass_on)
        at_step(t - 1, pass_far)
        at_step(t - 4, lambda g: (add_far(g, 0), add_far(g, 1)))
        at_step(t - 5, finish)
        at_step(t - 3, merge_all)
        at_step(t - 2, settle)
        at_step(t - 2, compute)

    loop(0, STEPS + 2, tick)

    for j in range(GROUPS):
        each = r.acc_k.shape[0] // GROUPS
        block = slice(each * j, each * j + each)
        r.gw[j] = jnp.concatenate([r.acc_k[block], r.acc_v[block]], axis=0).astype(jnp.bfloat16)

    def w_copy(d, dest):
        return remote(r.gw.at[dest], r.wsum.at[d], r.w_send.at[d], r.w_recv.at[d], (dest, ret))

    loop(1, GROUPS, lambda d: w_copy(d, ahead(seq, d)).start())
    r.wsum[0] = r.gw[seq]
    loop(STEPS + 2, STEPS + 5, tick)

    def back_copy(d, dest, slot):
        return remote(
            r.leaving_b.at[dest],
            r.arrived_b.at[slot],
            r.back_send.at[d],
            r.back_recv.at[d],
            (dest, ret),
        )

    def give_back(d):
        dest = ahead(seq, d)
        for k in range(CAP):
            r.leaving_b[dest, k] = r.total[r.source[dest * CAP + k]]
        back_copy(d, dest, seq).start()

    loop(1, GROUPS, give_back)
    for k in range(CAP):
        r.arrived_b[seq, k] = r.total[r.source[seq * CAP + k]]

    loop(1, GROUPS, lambda d: w_copy(d, ahead(seq, d)).wait())
    rows_w = r.gk_out.shape[0]
    for c in range(0, r.gk_out.shape[1], 128):
        col = pl.ds(c, 128)
        w_total = r.wsum[0, :, col].astype(jnp.float32)
        for d in range(1, GROUPS):
            w_total = w_total + r.wsum[d, :, col].astype(jnp.float32)
        r.gk_out[:, col] = w_total[:rows_w]
        r.gv_out[:, col] = w_total[rows_w:]

    loop(1, GROUPS, lambda d: back_copy(d, ahead(seq, d), behind(seq, d)).wait())

    def home_copy(d, dest, slot):
        return remote(
            r.table.at[pl.ds(2 * dest, 2)],
            r.home.at[:, slot],
            r.home_send.at[d],
            r.home_recv.at[d],
            (seq, dest),
        )

    def sum_slot(slot):
        def add(s, carry):
            for k in range(CAP):
                here = r.served_s[s, 0, k] == slot
                carry = carry + jnp.where(here, r.arrived_b[s, k].astype(jnp.float32), 0.0)
            return carry

        r.table[slot] = lax.fori_loop(0, GROUPS, add, jnp.zeros((16, feat), jnp.float32)).astype(
            jnp.bfloat16
        )

    def send_home(d):
        dest = (ret + d) % RETS
        sum_slot(2 * dest)
        sum_slot(2 * dest + 1)
        home_copy(d, dest, ret).start()

    loop(1, RETS, send_home)
    sum_slot(2 * ret)
    sum_slot(2 * ret + 1)
    for k in range(2):
        r.home[k, ret] = r.table[2 * ret + k]
    loop(1, RETS, lambda d: home_copy(d, (ret + d) % RETS, (ret + RETS - d) % RETS).wait())
    for g in range(STEPS):
        for copy in result_copies(g):
            copy.wait()


def attend(r, g, size):
    feat, width = r.wk.shape
    heads = width // HD
    spans = size // 2
    scale = 1.0 / math.sqrt(HD)
    rows = r.picked[pl.ds(g * size, size)].reshape(size * 128, feat)
    r.keys[...] = dot(rows, r.wk[...]).astype(jnp.bfloat16)
    r.values[...] = dot(rows, r.wv[...]).astype(jnp.bfloat16)
    for c in range(spans):
        tok = pl.ds(pl.multiple_of((g * spans + c) * 64, 64), 64)
        row = slice(256 * c, 256 * c + 256)
        for h in range(heads):
            col = slice(HD * h, HD * h + HD)
            qh, gh = r.q[tok, col], r.go[tok, col]
            kh, vh = r.keys[row, col], r.values[row, col]
            weights = jnp.exp(dot(qh, kh, NT) * scale)
            weights = weights / jnp.sum(weights, axis=-1, keepdims=True)
            probs = weights.astype(jnp.bfloat16)
            r.ctx[tok, col] = dot(probs, vh).astype(jnp.bfloat16)
            gp = dot(gh, vh, NT)
            mixed = (
                weights * (gp - jnp.sum(weights * gp, axis=-1, keepdims=True)) * scale
            ).astype(jnp.bfloat16)
            r.gq[tok, col] = dot(mixed, kh).astype(jnp.bfloat16)
            r.gkeys[row, col] = dot(mixed, qh, TN).astype(jnp.bfloat16)
            r.gvalues[row, col] = dot(probs, gh, TN).astype(jnp.bfloat16)
    part = dot(r.gkeys[...], r.wk[...], NT) + dot(r.gvalues[...], r.wv[...], NT)
    r.part[pl.ds(g * size, size)] = part.astype(jnp.bfloat16).reshape(size, SIDE, 2, 16, feat)
    add_k = dot(rows, r.gkeys[...], TN)
    add_v = dot(rows, r.gvalues[...], TN)

    @pl.when(g == 0)
    def _():
        r.acc_k[...] = add_k
        r.acc_v[...] = add_v

    @pl.when(g > 0)
    def _():
        r.acc_k[...] += add_k
        r.acc_v[...] += add_v


def fused(
    queries,
    grad_ctx,
    neighbours,
    up_weight,
    down_weight,
    key_weight,
    value_weight,
    wanted,
    position,
    source,
):
    feat, ffe = up_weight.shape
    requests = position.shape[0]
    tokens, width = queries.shape
    size = requests // STEPS
    bf, f32 = jnp.bfloat16, jnp.float32
    dma = pltpu.SemaphoreType.DMA
    slots = (GROUPS, CAP, 16, feat)
    chunk = (requests, 16, feat)
    any_, vmem, smem = (
        pl.BlockSpec(memory_space=s) for s in (pl.ANY, pltpu.VMEM, pltpu.SMEM)
    )
    ins = dict(
        queries=any_,
        grad_ctx=any_,
        neighbours=any_,
        up_weight=any_,
        down_weight=any_,
        key_weight=any_,
        value_weight=any_,
        wanted=vmem,
        position=smem,
        source=smem,
    )
    outs = dict(
        context=(any_, queries.shape, bf),
        grad_query=(any_, queries.shape, bf),
        home=(vmem, (2, RETS, 16, feat), bf),
        gk_out=(vmem, (feat // GROUPS, width), f32),
        gv_out=(vmem, (feat // GROUPS, width), f32),
    )
    scratch = dict(
        served=pltpu.VMEM(wanted.shape, jnp.int32),
        served_s=pltpu.SMEM(wanted.shape, jnp.int32),
        raw=pltpu.VMEM((2 * RETS, 16, feat), bf),
        normed=pltpu.VMEM((2 * RETS * 16, feat), bf),
        encoding=pltpu.VMEM((2 * RETS * 16, feat), f32),
        up_w=pltpu.VMEM((BLOCKS, feat, ffe // BLOCKS), bf),
        down_w=pltpu.VMEM((BLOCKS, ffe // BLOCKS, feat), bf),
        table=pltpu.VMEM((2 * RETS, 16, feat), bf),
        arrived=pltpu.VMEM(slots, bf),
        leaving=pltpu.VMEM(slots, bf),
        own=pltpu.VMEM(chunk, bf),
        picked=pltpu.VMEM((requests, RETS, 16, feat), bf),
        wk=pltpu.VMEM((feat, width), bf),
        wv=pltpu.VMEM((feat, width), bf),
        q=pltpu.VMEM(queries.shape, bf),
        go=pltpu.VMEM(queries.shape, bf),
        ctx=pltpu.VMEM(queries.shape, bf),
        gq=pltpu.VMEM(queries.shape, bf),
        keys=pltpu.VMEM((size * 128, width), bf),
        values=pltpu.VMEM((size * 128, width), bf),
        gkeys=pltpu.VMEM((size * 128, width), bf),
        gvalues=pltpu.VMEM((size * 128, width), bf),
        acc_k=pltpu.VMEM((feat, width), f32),
        acc_v=pltpu.VMEM((feat, width), f32),
        part=pltpu.VMEM((requests, SIDE, 2, 16, feat), bf),
        sib=pltpu.VMEM((SIDE,) + chunk, bf),
        far=pltpu.VMEM(chunk, bf),
        near_up=pltpu.VMEM(chunk, bf),
        near_down=pltpu.VMEM(chunk, bf),
        total=pltpu.VMEM(chunk, bf),
        leaving_b=pltpu.VMEM(slots, bf),
        arrived_b=pltpu.VMEM(slots, bf),
        gw=pltpu.VMEM((GROUPS, 2 * feat // GROUPS, width), bf),
        wsum=pltpu.VMEM((GROUPS, 2 * feat // GROUPS, width), bf),
        up_sem=dma((BLOCKS,)),
        down_sem=dma((BLOCKS,)),
        load_sem=dma((5,)),
        scalar_sem=dma,
        keep_sem=dma((STEPS,)),
        out_sem=dma((STEPS, 2)),
    )
    for name, shape in dict(
        id=(GROUPS,),
        raw=(RETS,),
        seq=(GROUPS,),
        up=(STEPS, 2),
        dn=(STEPS, 2),
        far=(STEPS, 2),
        sib=(STEPS, 4),
        swap=(STEPS, 4),
        rfar=(STEPS, 2),
        rup=(STEPS, 2),
        rdn=(STEPS, 2),
        w=(GROUPS,),
        back=(GROUPS,),
        home=(RETS,),
    ).items():
        scratch[name + "_send"] = dma(shape)
        scratch[name + "_recv"] = dma(shape)
    names = tuple(ins) + tuple(outs) + tuple(scratch)
    return pl.pallas_call(
        functools.partial(kernel, names),
        out_shape=tuple(jax.ShapeDtypeStruct(s, t) for _, s, t in outs.values()),
        in_specs=list(ins.values()),
        out_specs=tuple(s for s, _, _ in outs.values()),
        scratch_shapes=list(scratch.values()),
        compiler_params=pltpu.CompilerParams(
            collective_id=0, has_side_effects=True, vmem_limit_bytes=60 * MIB
        ),
        name="fused",
    )(
        queries,
        grad_ctx,
        neighbours.reshape(2, RETS, 16, feat),
        up_weight,
        down_weight,
        key_weight,
        value_weight,
        wanted,
        position,
        source,
    )


def body(
    queries,
    grad_ctx,
    neighbours,
    up_weight,
    down_weight,
    key_weight,
    value_weight,
    group_ids,
    slot_ids,
):
    targets, slots = group_ids.reshape(-1), slot_ids.reshape(-1)
    requests = targets.shape[0]
    order = jnp.arange(requests, dtype=jnp.int32)
    earlier = (targets[:, None] == targets[None, :]) & (order[None, :] < order[:, None])
    position = targets * CAP + jnp.sum(earlier.astype(jnp.int32), axis=1)
    match = position[:, None] == jnp.arange(GROUPS * CAP, dtype=jnp.int32)[None, :]
    wanted = jnp.sum(jnp.where(match, slots[:, None] + 1, 0), axis=0) - 1
    source = jnp.sum(jnp.where(match, order[:, None], 0), axis=0)
    wanted = jnp.pad(wanted.reshape(GROUPS, 1, CAP), ((0, 0), (0, 7), (0, 128 - CAP)))
    context, grad_query, home, grad_key_w, grad_value_w = fused(
        queries,
        grad_ctx,
        neighbours,
        up_weight,
        down_weight,
        key_weight,
        value_weight,
        wanted,
        position,
        source,
    )
    return context, grad_query, home.reshape(neighbours.shape), grad_key_w, grad_value_w


def solution(mesh):
    return jax.shard_map(
        body,
        mesh=mesh,
        in_specs=(
            P("seq", "ret"),
            P("seq", "ret"),
            P(("seq", "ret"), None, None),
            P(),
            P(),
            P(None, "ret"),
            P(None, "ret"),
            P("seq", None),
            P("seq", None),
        ),
        out_specs=(
            P("seq", "ret"),
            P("seq", "ret"),
            P(("seq", "ret"), None, None),
            P("seq", "ret"),
            P("seq", "ret"),
        ),
        check_vma=False,
    )
```

time: 930 us -> 184 us (0.20)
  waiting for transfers between devices: 546 us -> 0 us
  local copies, waits for them, and re-layouts: 208 us -> 10.8 us
  Pallas kernels: 0 us -> 171 us
  matrix products: 106 us -> 0 us
  other arithmetic: 22.4 us -> 1.47 us
  blocking collectives: 13.8 us -> 0 us
  between operations: 14.3 us -> 0.66 us
  starting transfers between devices: 12.6 us -> 0 us
    all_to_all x2 -> x0, waiting for transfers between devices: 379 us -> none  [the longest x1 215 us: body(): lax.all_to_all(placed.reshape(groups, capacity, row_len * feat_width), 's...]
    pallas_call x0 -> x1, Pallas kernels: none -> 171 us  [fused(): pl.pallas_call(functools.partial(kernel, names), out_shape=tuple((jax.Sha...]
    unnamed x6 -> x0, waiting for transfers between devices: 150 us -> none
    scatter x2 -> x0, local copies, waits for them, and re-layouts: 109 us -> none  [the longest x1 109 us: body(): placed = jnp.zeros((slot_total, row_len * feat_width), jnp.bfloat16).at[p...]
    dot_general x14 -> x0, matrix products: 106 us -> none  [the longest x1 24.5 us: attend(): jnp.einsum('chqk,cqhd->ckhd', mixed, queries, preferred_element_type=jnp....]
    reshape x12 -> x1, local copies, waits for them, and re-layouts: 57.4 us -> 0.08 us  [body(): targets, slots = (group_ids.reshape(-1), slot_ids.reshape(-1))]
    gather x2 -> x0, local copies, waits for them, and re-layouts: 17.3 us -> none  [the longest x1 9.26 us: body(): source_rows = jnp.take(enc_table, served, axis=0)]
    all_gather x1 -> x0, waiting for transfers between devices: 17 us -> none  [full_table(): return lax.all_gather(encoded_own, 'ret', axis=0, tiled=True)]
  transfers between devices with their start and end apart: 6 -> 0, of which waited for: 5 -> 0; matrix products, arithmetic and copies ran while one was open for 5% -> 0% of each run, Pallas kernels for 0% -> 0%
where the time goes in v2:
time: 184 us
  Pallas kernels  171 us (93%)
  local copies, waits for them, and re-layouts  10.8 us (6%)
    pallas_call x1, Pallas kernels, fused(): pl.pallas_call(functools.partial(kernel, names), out_shape=tuple((jax.Sha...  171 us
    unnamed x8, local copies, waits for them, and re-layouts  9.83 us

profile of v2, /device:TPU:1, one launch (start us, length us, event | category | flops | bytes accessed | tf_op | source)
XLA Modules:
  0.0 183.6 jit_solution(9019970112843810804)
XLA Ops:
  0.6 0.7 broadcast_add_fusion
  1.3 0.1 copy.21
  1.4 0.1 add.27
  1.5 0.8 copy.20
  2.3 0.1 reshape.52
  2.4 0.2 convert_reduce_fusion
  2.5 0.0 copy-start
  2.6 0.6 select_reduce_fusion
  3.2 0.1 sub.7
  3.2 0.6 pad.4.refs_7_
  3.9 0.0 copy-done
  3.9 170.6 %fused.1 = (bf16[768,512]{1,0:T(8,128)(2,1)}, bf16[768,512]{1,0:T(8,128)(2,1)}, bf16[2,8,16,896]{3,2,1,0:T(8,128)(2,1)}, f32[56,512]{1,0:T(8,128)}, f32[56,512]{1,0:T(8,128)}) custom-call(bf16[768,512]{1,0:T(8,128)(2,1)} %refs_0_.1, bf16[768,512]{1,0:T(8,128)(2,1)} %refs_1_.1, bf16[2,8,16,896]{3,2,1,0:T(8,128)(2,1)} %bitcast.4, bf16[896,3584]{1,0:T(8,128)(2,1)} %refs_3_.1, ...), custom_call_target="tpu_custom_call" | custom-call | tf_op jit(solution)/shard_map/fused/pallas_call | solution.py:617
  174.6 2.1 %copy.28 = bf16[768,512]{1,0:T(8,128)(2,1)} copy(bf16[768,512]{1,0:T(8,128)(2,1)} %get-tuple-element.22) | data formatting | bytes 1572864
  176.6 2.1 %copy.29 = bf16[768,512]{1,0:T(8,128)(2,1)} copy(bf16[768,512]{1,0:T(8,128)(2,1)} %get-tuple-element.23) | data formatting | bytes 1572864
  178.7 1.8 copy.30
  180.5 1.6 copy.31
  182.1 1.6 copy.32
  (2 shorter events, 0.0 us)
Async XLA Ops:
  2.5 1.4 copy-start

commit v3 on v2

v3 whole, which is shorter than its diff:
```python
import functools
import math

import jax
import jax.numpy as jnp
from jax import lax
from jax.experimental import pallas as pl
from jax.experimental.pallas import tpu as pltpu
from jax.sharding import PartitionSpec as P

HD = 128
CAP = 3
MESH = pl.DeviceIdType.MESH
SIDE = 4
GROUPS = 16
RETS = 8
STEPS = 6
BLOCKS = 7
CUT = 512
EARLY = 2
MIB = 1024 * 1024


def ahead(seq, d):
    y, x = seq // SIDE, seq % SIDE
    return ((y + d // SIDE) % SIDE) * SIDE + (x + d % SIDE) % SIDE


def behind(seq, d):
    y, x = seq // SIDE, seq % SIDE
    return ((y + SIDE - d // SIDE) % SIDE) * SIDE + (x + SIDE - d % SIDE) % SIDE


def loop(low, high, step):
    def run(i, carry):
        step(i)
        return carry

    lax.fori_loop(low, high, run, 0)


def greet(seq, ret):
    barrier = pltpu.get_barrier_semaphore()

    def to_seq(d):
        pl.semaphore_signal(barrier, inc=1, device_id=(ahead(seq, d), ret), device_id_type=MESH)

    def to_ret(d):
        pl.semaphore_signal(barrier, inc=1, device_id=(seq, (ret + d) % RETS), device_id_type=MESH)

    loop(1, GROUPS, to_seq)
    loop(1, RETS, to_ret)
    return lambda: pl.semaphore_wait(barrier, GROUPS + RETS - 2)


def remote(src, dst, send, recv, to):
    return pltpu.make_async_remote_copy(
        src_ref=src,
        dst_ref=dst,
        send_sem=send,
        recv_sem=recv,
        device_id=to,
        device_id_type=MESH,
    )


NT = (((1,), (1,)), ((), ()))
TN = (((0,), (0,)), ((), ()))


def dot(a, b, dims=(((1,), (0,)), ((), ()))):
    return lax.dot_general(a, b, dims, preferred_element_type=jnp.float32)


class Refs:
    def __init__(self, names, refs):
        self.__dict__.update(zip(names, refs))


def kernel(names, *refs):
    r = Refs(names, refs)
    seq, ret = lax.axis_index("seq"), lax.axis_index("ret")
    z, core = ret // 2, ret % 2
    above, below, facing = (z + 1) % SIDE, (z + SIDE - 1) % SIDE, (z + 2) % SIDE
    sibling = (seq, 2 * z + 1 - core)
    up_to, down_to = (seq, 2 * above + core), (seq, 2 * below + core)
    requests = r.own.shape[0]
    size = requests // STEPS
    half = size // 2
    feat = r.own.shape[-1]

    def up_load(j):
        width = r.up_w.shape[-1]
        return pltpu.make_async_copy(
            r.up_weight.at[:, pl.ds(j * width, width)], r.up_w.at[j], r.up_sem.at[j]
        )

    def down_load(j):
        depth = r.down_w.shape[1]
        return pltpu.make_async_copy(
            r.down_weight.at[pl.ds(j * depth, depth)], r.down_w.at[j], r.down_sem.at[j]
        )

    loads = [
        pltpu.make_async_copy(a, b, r.load_sem.at[i])
        for i, (a, b) in enumerate(
            (
                (r.key_weight, r.wk),
                (r.value_weight, r.wv),
                (r.queries, r.q),
                (r.grad_ctx, r.go),
                (r.neighbours, r.raw),
            )
        )
    ]
    loads[4].start()
    for j in range(BLOCKS):
        up_load(j).start()
        down_load(j).start()
    for i in range(4):
        loads[i].start()

    greeted = greet(seq, ret)

    targets = [r.group_ids[i % 2, i // 2] for i in range(requests)]
    slots = [r.slot_ids[i % 2, i // 2] for i in range(requests)]
    lane = lax.broadcasted_iota(jnp.int32, (8, 128), 1)
    wanted = jnp.full((8, 128), -1, jnp.int32)
    source = jnp.zeros((8, 128), jnp.int32)
    for i in range(requests):
        count = jnp.int32(0)
        for j in range(i):
            count += (targets[j] == targets[i]).astype(jnp.int32)
        at = targets[i] * CAP + count
        r.position[i] = at
        wanted = jnp.where(lane == at, slots[i], wanted)
        source = jnp.where(lane == at, i, source)
    r.wanted[...] = wanted
    r.source_v[...] = source
    to_source = pltpu.make_async_copy(r.source_v, r.source, r.scalar_sem.at[1])
    to_source.start()

    loads[4].wait()
    inputs = r.raw[...].reshape(-1, feat).astype(jnp.float32)
    normed = inputs * lax.rsqrt(jnp.mean(inputs * inputs, axis=-1, keepdims=True) + 1e-06)
    r.normed[...] = normed.astype(jnp.bfloat16)
    r.encoding[...] = inputs

    def feed(j):
        up_load(j).wait()
        hidden = jax.nn.gelu(dot(r.normed[...], r.up_w[j])).astype(jnp.bfloat16)
        down_load(j).wait()
        r.encoding[...] += dot(hidden, r.down_w[j])

    loop(0, BLOCKS, feed)
    r.enc[...] = r.encoding[...].astype(jnp.bfloat16).reshape(r.enc.shape)
    to_source.wait()
    greeted()

    def id_copy(d, dest, slot):
        return remote(r.wanted, r.served.at[slot], r.id_send.at[d], r.id_recv.at[d], (dest, ret))

    def slice_copy(d, dest, slot):
        return remote(
            r.enc.at[:, dest],
            r.table.at[pl.ds(2 * slot, 2)],
            r.raw_send.at[d],
            r.raw_recv.at[d],
            (seq, dest),
        )

    loop(1, RETS, lambda d: slice_copy(d, (ret + d) % RETS, ret).start())
    loop(1, GROUPS, lambda d: id_copy(d, ahead(seq, d), seq).start())
    r.served[seq] = wanted
    for k in range(2):
        r.table[2 * ret + k] = r.enc[k, ret]
    loop(1, GROUPS, lambda d: id_copy(d, ahead(seq, d), behind(seq, d)).wait())
    to_scalar = pltpu.make_async_copy(r.served, r.served_s, r.scalar_sem.at[0])
    to_scalar.start()
    to_scalar.wait()
    loop(1, RETS, lambda d: slice_copy(d, (ret + d) % RETS, (ret + RETS - d) % RETS).wait())

    def asked(s, k):
        return r.served_s[s, 0, seq * CAP + k]

    def seq_copy(d, dest, slot):
        return remote(
            r.leaving.at[dest], r.arrived.at[slot], r.seq_send.at[d], r.seq_recv.at[d], (dest, ret)
        )

    def serve(d):
        dest = ahead(seq, d)
        for k in range(CAP):
            r.leaving[dest, k] = r.table[jnp.maximum(asked(dest, k), 0)]
        seq_copy(d, dest, seq).start()

    loop(1, GROUPS, serve)
    for k in range(CAP):
        r.arrived[seq, k] = r.table[jnp.maximum(asked(seq, k), 0)]
    loop(1, GROUPS, lambda d: seq_copy(d, ahead(seq, d), behind(seq, d)).wait())

    def compact(i):
        at = r.position[i]
        r.own[i] = r.arrived[at // CAP, at % CAP]

    loop(0, requests, compact)
    for i in range(4):
        loads[i].wait()

    def rows(g, h):
        return pl.ds(g * size + h * half, half)

    def own_up(g, h, held):
        return remote(
            r.own.at[rows(g, h)],
            r.picked.at[rows(g, h), 2 * held + core],
            r.up_send.at[g, h],
            r.up_recv.at[g, h],
            up_to,
        )

    def own_down(g, h, held):
        return remote(
            r.own.at[rows(g, h)],
            r.picked.at[rows(g, h), 2 * held + core],
            r.dn_send.at[g, h],
            r.dn_recv.at[g, h],
            down_to,
        )

    def relay(g, h, held):
        return remote(
            r.picked.at[rows(g, h), 2 * held + core],
            r.picked.at[rows(g, h), 2 * held + core],
            r.far_send.at[g, h],
            r.far_recv.at[g, h],
            down_to if h else up_to,
        )

    def across(g, o, held, side):
        whole = pl.ds(g * size, size)
        source = r.picked.at[whole, 2 * held + side]
        return remote(
            r.own.at[whole] if o == 0 else source,
            source,
            r.sib_send.at[g, o],
            r.sib_recv.at[g, o],
            sibling,
        )

    def keep(g):
        whole = pl.ds(g * size, size)
        return pltpu.make_async_copy(
            r.own.at[whole], r.picked.at[whole, ret], r.keep_sem.at[g]
        )

    def send_own(g):
        own_up(g, 0, z).start()
        own_down(g, 1, z).start()
        own_up(g, 1, z).start()
        own_down(g, 0, z).start()
        across(g, 0, z, core).start()
        keep(g).start()

    def pass_on(g):
        own_up(g, 0, below).wait_recv()
        relay(g, 0, below).start()
        own_down(g, 1, above).wait_recv()
        relay(g, 1, above).start()
        own_up(g, 1, below).wait_recv()
        across(g, 1, below, core).start()
        own_down(g, 0, above).wait_recv()
        across(g, 2, above, core).start()

    def pass_far(g):
        relay(g, 0, facing).wait_recv()
        relay(g, 1, facing).wait_recv()
        across(g, 3, facing, core).start()

    def settle(g):
        for h in range(2):
            own_up(g, h, z).wait_send()
            own_down(g, h, z).wait_send()
            relay(g, h, above if h else below).wait_send()
        keep(g).wait()
        across(g, 0, z, 1 - core).wait()
        across(g, 1, below, 1 - core).wait()
        across(g, 2, above, 1 - core).wait()
        across(g, 3, facing, 1 - core).wait()

    cols = (pl.ds(0, CUT), pl.ds(CUT, feat - CUT))

    def swap(p, g, o):
        whole = pl.ds(g * size, size)
        return remote(
            r.part.at[whole, (z + o) % SIDE, 1 - core, :, cols[p]],
            r.sib.at[o, whole, :, cols[p]],
            r.swap_send.at[p, g, o],
            r.swap_recv.at[p, g, o],
            sibling,
        )

    def ring_copy(name, dst, at, to):
        send, recv = getattr(r, name + "_send"), getattr(r, name + "_recv")

        def copy(p, g, h):
            return remote(
                r.part.at[rows(g, h), at, core, :, cols[p]],
                dst.at[rows(g, h), :, cols[p]],
                send.at[p, g, h],
                recv.at[p, g, h],
                to(h),
            )

        return copy

    far_copy = ring_copy("rfar", r.far, facing, lambda h: down_to if h else up_to)
    up_copy = ring_copy("rup", r.near_up, above, lambda h: up_to)
    down_copy = ring_copy("rdn", r.near_down, below, lambda h: down_to)

    def merge(p, g, o):
        swap(p, g, o).wait_recv()
        at = (z + o) % SIDE
        whole = pl.ds(g * size, size)
        mine = r.part[whole, at, core, :, cols[p]].astype(jnp.float32)
        other = r.sib[o, whole, :, cols[p]].astype(jnp.float32)
        r.part[whole, at, core, :, cols[p]] = (mine + other).astype(jnp.bfloat16)

    def merge_all(p, g):
        merge(p, g, 2)
        far_copy(p, g, 0).start()
        far_copy(p, g, 1).start()
        merge(p, g, 1)
        up_copy(p, g, 1).start()
        merge(p, g, 3)
        down_copy(p, g, 0).start()
        merge(p, g, 0)

    def add_far(p, g):
        for h in range(2):
            far_copy(p, g, h).wait_recv()
            at = below if h else above
            mine = r.part[rows(g, h), at, core, :, cols[p]].astype(jnp.float32)
            other = r.far[rows(g, h), :, cols[p]].astype(jnp.float32)
            r.part[rows(g, h), at, core, :, cols[p]] = (mine + other).astype(jnp.bfloat16)
            (down_copy if h else up_copy)(p, g, h).start()

    def finish(p, g):
        for h in range(2):
            up_copy(p, g, h).wait_recv()
            down_copy(p, g, h).wait_recv()
        whole = pl.ds(g * size, size)
        r.total[whole, :, cols[p]] = (
            r.part[whole, z, core, :, cols[p]].astype(jnp.float32)
            + r.near_up[whole, :, cols[p]].astype(jnp.float32)
            + r.near_down[whole, :, cols[p]].astype(jnp.float32)
        ).astype(jnp.bfloat16)
        for o in range(4):
            swap(p, g, o).wait_send()
        for h in range(2):
            far_copy(p, g, h).wait_send()
            up_copy(p, g, h).wait_send()
            down_copy(p, g, h).wait_send()

    def project(p, g):
        gk, gv = r.up_w[g, : size * 128, :], r.down_w[g, :, : r.wk.shape[1]]
        part = dot(gk, r.wk[cols[p], :], NT) + dot(gv, r.wv[cols[p], :], NT)
        r.part[pl.ds(g * size, size), :, :, :, cols[p]] = part.astype(jnp.bfloat16).reshape(
            size, SIDE, 2, 16, part.shape[1]
        )
        for o in (2, 1, 3, 0):
            swap(p, g, o).start()

    def result_copies(g):
        tokens = pl.ds(g * (size * 32), size * 32)
        return (
            pltpu.make_async_copy(r.ctx.at[tokens], r.context.at[tokens], r.out_sem.at[g, 0]),
            pltpu.make_async_copy(r.gq.at[tokens], r.grad_query.at[tokens], r.out_sem.at[g, 1]),
        )

    def compute(g):
        attend(r, g, size)
        for copy in result_copies(g):
            copy.start()

    def at_step(g, step):
        @pl.when((g >= 0) & (g < STEPS))
        def _():
            step(g)

    for g in range(EARLY):
        send_own(g)

    def tick(t):
        at_step(t + EARLY, send_own)
        at_step(t, pass_on)
        at_step(t - 1, pass_far)
        at_step(t - 2, settle)
        at_step(t - 2, compute)

    loop(0, STEPS + 2, tick)

    y, x = seq // SIDE, seq % SIDE
    each = feat // GROUPS
    wide = r.acc_k.shape[1] // 2
    for j in range(GROUPS):
        block = slice(each * j, each * j + each)
        for h in range(2):
            col = slice(wide * h, wide * h + wide)
            r.gw[j // SIDE, j % SIDE, h] = jnp.concatenate(
                [r.acc_k[block, col], r.acc_v[block, col]], axis=0
            ).astype(jnp.bfloat16)

    def along_x(d):
        return (y * SIDE + (x + d) % SIDE, ret)

    def along_y(d):
        return (((y + d) % SIDE) * SIDE + x, ret)

    def w_copy(h, d):
        return remote(
            r.gw.at[(y + d) % SIDE, :, 1] if h else r.gw.at[:, (x + d) % SIDE, 0],
            r.w_in.at[h, d],
            r.w_send.at[h, d],
            r.w_recv.at[h, d],
            along_y(d) if h else along_x(d),
        )

    def w_last(h, d):
        return remote(
            r.w_half.at[h, (x + d) % SIDE if h else (y + d) % SIDE],
            r.w_end.at[h, d],
            r.w2_send.at[h, d],
            r.w2_recv.at[h, d],
            along_x(d) if h else along_y(d),
        )

    def w_middle():
        for h in range(2):
            for d in range(1, SIDE):
                w_copy(h, d).wait()
            for j in range(SIDE):
                mine = r.gw[y, j, 1] if h else r.gw[j, x, 0]
                summed = mine.astype(jnp.float32)
                for d in range(1, SIDE):
                    summed = summed + r.w_in[h, d, j].astype(jnp.float32)
                r.w_half[h, j] = summed.astype(jnp.bfloat16)
            for d in range(1, SIDE):
                w_last(h, d).start()

    for d in range(1, SIDE):
        for h in range(2):
            w_copy(h, d).start()

    def back_copy(p, d, dest, slot):
        return remote(
            r.leaving.at[dest, :, :, cols[p]],
            r.arrived_b.at[slot, :, :, cols[p]],
            r.back_send.at[p, d],
            r.back_recv.at[p, d],
            (dest, ret),
        )

    def give_back(p):
        def give(d):
            dest = ahead(seq, d)
            for k in range(CAP):
                r.leaving[dest, k, :, cols[p]] = r.total[r.source[0, dest * CAP + k], :, cols[p]]
            back_copy(p, d, dest, seq).start()

        loop(1, GROUPS, give)
        for k in range(CAP):
            r.arrived_b[seq, k, :, cols[p]] = r.total[r.source[0, seq * CAP + k], :, cols[p]]

    def tock(t):
        for p in range(2):
            begin = p * STEPS
            at_step(t - begin - 5, lambda g: finish(p, g))
            at_step(t - begin - 3, lambda g: add_far(p, g))
            at_step(t - begin - 1, lambda g: merge_all(p, g))
            at_step(t - begin, lambda g: project(p, g))
        pl.when(t == STEPS)(w_middle)
        pl.when(t == STEPS + 4)(lambda: give_back(0))

    loop(0, 2 * STEPS + 5, tock)
    give_back(1)

    row = lax.broadcasted_iota(jnp.int32, r.pick.shape, 0)
    col = lax.broadcasted_iota(jnp.int32, r.pick.shape, 1)
    place = lax.broadcasted_iota(jnp.int32, (1, r.pick.shape[1]), 1) // 16
    owner = jnp.full(place.shape, -1, jnp.int32)
    for s in range(GROUPS):
        for k in range(CAP):
            owner = jnp.where(place == s * CAP + k, asked(s, k), owner)
    r.pick[...] = jnp.where((row // 16 == owner) & (row % 16 == col % 16), 1.0, 0.0).astype(
        jnp.bfloat16
    )

    def home_copy(p, d, dest, slot):
        return remote(
            r.table.at[pl.ds(2 * dest, 2), :, cols[p]],
            r.home.at[:, slot, :, cols[p]],
            r.home_send.at[p, d],
            r.home_recv.at[p, d],
            (seq, dest),
        )

    def go_home(p):
        loop(1, GROUPS, lambda d: back_copy(p, d, ahead(seq, d), behind(seq, d)).wait())
        arrived = r.arrived_b[:, :, :, cols[p]]
        summed = dot(r.pick[...], arrived.reshape(r.pick.shape[1], arrived.shape[-1]))
        r.table[:, :, cols[p]] = summed.astype(jnp.bfloat16).reshape(
            2 * RETS, 16, arrived.shape[-1]
        )
        loop(1, RETS, lambda d: home_copy(p, d, (ret + d) % RETS, ret).start())
        for k in range(2):
            r.home[k, ret, :, cols[p]] = r.table[2 * ret + k, :, cols[p]]

    go_home(0)
    for h in range(2):
        summed = r.w_half[h, x if h else y].astype(jnp.float32)
        for d in range(1, SIDE):
            w_last(h, d).wait()
            summed = summed + r.w_end[h, d].astype(jnp.float32)
        r.gk_out[:, wide * h : wide * h + wide] = summed[:each]
        r.gv_out[:, wide * h : wide * h + wide] = summed[each:]
    go_home(1)
    for p in range(2):
        loop(
            1,
            RETS,
            lambda d: home_copy(p, d, (ret + d) % RETS, (ret + RETS - d) % RETS).wait(),
        )
    for g in range(STEPS):
        for copy in result_copies(g):
            copy.wait()


def attend(r, g, size):
    feat, width = r.wk.shape
    heads = width // HD
    spans = size // 2
    scale = 1.0 / math.sqrt(HD)
    rows = r.picked[pl.ds(g * size, size)].reshape(size * 128, feat)
    r.keys[...] = dot(rows, r.wk[...]).astype(jnp.bfloat16)
    r.values[...] = dot(rows, r.wv[...]).astype(jnp.bfloat16)
    gkeys, gvalues = r.up_w.at[g, : size * 128], r.down_w.at[g, :, :width]
    for c in range(spans):
        tok = pl.ds(pl.multiple_of((g * spans + c) * 64, 64), 64)
        row = slice(256 * c, 256 * c + 256)
        cols = [slice(HD * h, HD * h + HD) for h in range(heads)]
        scores = [dot(r.q[tok, col], r.keys[row, col], NT) for col in cols]
        gps = [dot(r.go[tok, col], r.values[row, col], NT) for col in cols]
        weights = [jnp.exp(s * scale) for s in scores]
        weights = [w / jnp.sum(w, axis=-1, keepdims=True) for w in weights]
        probs = [w.astype(jnp.bfloat16) for w in weights]
        mixed = [
            (w * (gp - jnp.sum(w * gp, axis=-1, keepdims=True)) * scale).astype(jnp.bfloat16)
            for w, gp in zip(weights, gps)
        ]
        for col, p, m in zip(cols, probs, mixed):
            r.ctx[tok, col] = dot(p, r.values[row, col]).astype(jnp.bfloat16)
            r.gq[tok, col] = dot(m, r.keys[row, col]).astype(jnp.bfloat16)
            gkeys[row, col] = dot(m, r.q[tok, col], TN).astype(jnp.bfloat16)
            gvalues[row, col] = dot(p, r.go[tok, col], TN).astype(jnp.bfloat16)
    add_k = dot(rows, gkeys[...], TN)
    add_v = dot(rows, gvalues[...], TN)

    @pl.when(g == 0)
    def _():
        r.acc_k[...] = add_k
        r.acc_v[...] = add_v

    @pl.when(g > 0)
    def _():
        r.acc_k[...] += add_k
        r.acc_v[...] += add_v


def fused(
    queries,
    grad_ctx,
    neighbours,
    up_weight,
    down_weight,
    key_weight,
    value_weight,
    group_ids,
    slot_ids,
):
    feat, ffe = up_weight.shape
    requests = group_ids.shape[0] * group_ids.shape[1]
    tokens, width = queries.shape
    size = requests // STEPS
    bf, f32 = jnp.bfloat16, jnp.float32
    dma = pltpu.SemaphoreType.DMA
    slots = (GROUPS, CAP, 16, feat)
    chunk = (requests, 16, feat)
    block = (2 * feat // GROUPS, width // 2)
    any_, vmem, smem = (
        pl.BlockSpec(memory_space=s) for s in (pl.ANY, pltpu.VMEM, pltpu.SMEM)
    )
    ins = dict(
        queries=any_,
        grad_ctx=any_,
        neighbours=any_,
        up_weight=any_,
        down_weight=any_,
        key_weight=any_,
        value_weight=any_,
        group_ids=smem,
        slot_ids=smem,
    )
    outs = dict(
        context=(any_, queries.shape, bf),
        grad_query=(any_, queries.shape, bf),
        home=(vmem, (2, RETS, 16, feat), bf),
        gk_out=(vmem, (feat // GROUPS, width), f32),
        gv_out=(vmem, (feat // GROUPS, width), f32),
    )
    scratch = dict(
        wanted=pltpu.VMEM((8, 128), jnp.int32),
        source_v=pltpu.VMEM((8, 128), jnp.int32),
        source=pltpu.SMEM((8, 128), jnp.int32),
        position=pltpu.SMEM((requests,), jnp.int32),
        served=pltpu.VMEM((GROUPS, 8, 128), jnp.int32),
        served_s=pltpu.SMEM((GROUPS, 8, 128), jnp.int32),
        raw=pltpu.VMEM((2, RETS, 16, feat), bf),
        enc=pltpu.VMEM((2, RETS, 16, feat), bf),
        normed=pltpu.VMEM((2 * RETS * 16, feat), bf),
        encoding=pltpu.VMEM((2 * RETS * 16, feat), f32),
        up_w=pltpu.VMEM((BLOCKS, feat, ffe // BLOCKS), bf),
        down_w=pltpu.VMEM((BLOCKS, ffe // BLOCKS, feat), bf),
        table=pltpu.VMEM((2 * RETS, 16, feat), bf),
        arrived=pltpu.VMEM(slots, bf),
        leaving=pltpu.VMEM(slots, bf),
        own=pltpu.VMEM(chunk, bf),
        picked=pltpu.VMEM((requests, RETS, 16, feat), bf),
        wk=pltpu.VMEM((feat, width), bf),
        wv=pltpu.VMEM((feat, width), bf),
        q=pltpu.VMEM(queries.shape, bf),
        go=pltpu.VMEM(queries.shape, bf),
        ctx=pltpu.VMEM(queries.shape, bf),
        gq=pltpu.VMEM(queries.shape, bf),
        keys=pltpu.VMEM((size * 128, width), bf),
        values=pltpu.VMEM((size * 128, width), bf),
        acc_k=pltpu.VMEM((feat, width), f32),
        acc_v=pltpu.VMEM((feat, width), f32),
        part=pltpu.VMEM((requests, SIDE, 2, 16, feat), bf),
        sib=pltpu.VMEM((SIDE,) + chunk, bf),
        far=pltpu.VMEM(chunk, bf),
        near_up=pltpu.VMEM(chunk, bf),
        near_down=pltpu.VMEM(chunk, bf),
        total=pltpu.VMEM(chunk, bf),
        arrived_b=pltpu.VMEM(slots, bf),
        gw=pltpu.VMEM((SIDE, SIDE, 2) + block, bf),
        w_in=pltpu.VMEM((2, SIDE, SIDE) + block, bf),
        w_half=pltpu.VMEM((2, SIDE) + block, bf),
        w_end=pltpu.VMEM((2, SIDE) + block, bf),
        pick=pltpu.VMEM((2 * RETS * 16, GROUPS * CAP * 16), bf),
        up_sem=dma((BLOCKS,)),
        down_sem=dma((BLOCKS,)),
        load_sem=dma((5,)),
        scalar_sem=dma((2,)),
        keep_sem=dma((STEPS,)),
        out_sem=dma((STEPS, 2)),
    )
    for name, shape in dict(
        id=(GROUPS,),
        raw=(RETS,),
        seq=(GROUPS,),
        up=(STEPS, 2),
        dn=(STEPS, 2),
        far=(STEPS, 2),
        sib=(STEPS, 4),
        swap=(2, STEPS, 4),
        rfar=(2, STEPS, 2),
        rup=(2, STEPS, 2),
        rdn=(2, STEPS, 2),
        w=(2, SIDE),
        w2=(2, SIDE),
        back=(2, GROUPS),
        home=(2, RETS),
    ).items():
        scratch[name + "_send"] = dma(shape)
        scratch[name + "_recv"] = dma(shape)
    names = tuple(ins) + tuple(outs) + tuple(scratch)
    return pl.pallas_call(
        functools.partial(kernel, names),
        out_shape=tuple(jax.ShapeDtypeStruct(s, t) for _, s, t in outs.values()),
        in_specs=list(ins.values()),
        out_specs=tuple(s for s, _, _ in outs.values()),
        scratch_shapes=list(scratch.values()),
        compiler_params=pltpu.CompilerParams(
            collective_id=0, has_side_effects=True, vmem_limit_bytes=60 * MIB
        ),
        name="fused",
    )(
        queries,
        grad_ctx,
        neighbours.reshape(2, RETS, 16, feat),
        up_weight,
        down_weight,
        key_weight,
        value_weight,
        group_ids,
        slot_ids,
    )


def deliver_kernel(*refs):
    count = len(refs) // 3
    sems = refs[-1]
    incoming = [
        pltpu.make_async_copy(refs[i], refs[2 * count + i], sems.at[0, i]) for i in range(count)
    ]
    outgoing = [
        pltpu.make_async_copy(refs[2 * count + i], refs[count + i], sems.at[1, i])
        for i in range(count)
    ]
    for copy in incoming:
        copy.start()
    for i in range(count):
        incoming[i].wait()
        outgoing[i].start()
    for copy in outgoing:
        copy.wait()


def deliver(arrays):
    any_ = pl.BlockSpec(memory_space=pl.ANY)
    return pl.pallas_call(
        deliver_kernel,
        out_shape=tuple(jax.ShapeDtypeStruct(a.shape, a.dtype) for a in arrays),
        in_specs=[any_] * len(arrays),
        out_specs=(any_,) * len(arrays),
        scratch_shapes=[pltpu.VMEM(a.shape, a.dtype) for a in arrays]
        + [pltpu.SemaphoreType.DMA((2, len(arrays)))],
        name="deliver",
    )(*arrays)


def body(
    queries,
    grad_ctx,
    neighbours,
    up_weight,
    down_weight,
    key_weight,
    value_weight,
    group_ids,
    slot_ids,
):
    context, grad_query, home, grad_key_w, grad_value_w = deliver(
        fused(
            queries,
            grad_ctx,
            neighbours,
            up_weight,
            down_weight,
            key_weight,
            value_weight,
            group_ids.T,
            slot_ids.T,
        )
    )
    return context, grad_query, home.reshape(neighbours.shape), grad_key_w, grad_value_w


def solution(mesh):
    return jax.shard_map(
        body,
        mesh=mesh,
        in_specs=(
            P("seq", "ret"),
            P("seq", "ret"),
            P(("seq", "ret"), None, None),
            P(),
            P(),
            P(None, "ret"),
            P(None, "ret"),
            P("seq", None),
            P("seq", None),
        ),
        out_specs=(
            P("seq", "ret"),
            P("seq", "ret"),
            P(("seq", "ret"), None, None),
            P("seq", "ret"),
            P("seq", "ret"),
        ),
        check_vma=False,
    )
```

time: 184 us -> 141 us (0.77)
  Pallas kernels: 171 us -> 140 us
  local copies, waits for them, and re-layouts: 10.8 us -> 0 us
    pallas_call x1, Pallas kernels: 171 us -> 137 us  [fused(): pl.pallas_call(functools.partial(kernel, names), out_shape=tuple((jax.Sha...]
    unnamed x8 -> x0, local copies, waits for them, and re-layouts: 9.83 us -> none
    pallas_call x0 -> x1, Pallas kernels: none -> 2.57 us  [deliver(): pl.pallas_call(deliver_kernel, out_shape=tuple((jax.ShapeDtypeStruct(a.sh...]
where the time goes in v3:
time: 141 us; the launch traced here: 140 us
  Pallas kernels  140 us (99%)
    pallas_call x1, Pallas kernels, fused(): pl.pallas_call(functools.partial(kernel, names), out_shape=tuple((jax.Sha...  137 us

profile of v3, /device:TPU:1, one launch (start us, length us, event | category | flops | bytes accessed | tf_op | source)
XLA Modules:
  0.0 140.5 jit_solution(12379501132056431202)
XLA Ops:
  0.6 137.2 %fused.1 = (bf16[768,512]{1,0:T(8,128)(2,1)}, bf16[768,512]{1,0:T(8,128)(2,1)}, bf16[2,8,16,896]{3,2,1,0:T(8,128)(2,1)}, f32[56,512]{1,0:T(8,128)}, f32[56,512]{1,0:T(8,128)}) custom-call(bf16[768,512]{1,0:T(8,128)(2,1)} %refs_0_.1, bf16[768,512]{1,0:T(8,128)(2,1)} %refs_1_.1, bf16[2,8,16,896]{3,2,1,0:T(8,128)(2,1)} %bitcast.4, bf16[896,3584]{1,0:T(8,128)(2,1)} %refs_3_.1, ...), custom_call_target="tpu_custom_call" | custom-call | tf_op jit(solution)/shard_map/fused/pallas_call | solution.py:688
  137.9 2.6 %deliver.1 = (bf16[768,512]{1,0:T(8,128)(2,1)}, bf16[768,512]{1,0:T(8,128)(2,1)}, bf16[2,8,16,896]{3,2,1,0:T(8,128)(2,1)}, f32[56,512]{1,0:T(8,128)}, f32[56,512]{1,0:T(8,128)}) custom-call(bf16[768,512]{1,0:T(8,128)(2,1)} %get-tuple-element.15.refs_0_, bf16[768,512]{1,0:T(8,128)(2,1)} %get-tuple-element.16.refs_1_, ...), custom_call_target="tpu_custom_call" | custom-call | tf_op jit(solution)/shard_map/deliver/pallas_call | solution.py:732

commit v4 on v3

--- a/solution.py
+++ b/solution.py
@@ -17,7 +17,10 @@
 STEPS = 6
 BLOCKS = 7
 CUT = 512
-EARLY = 2
+EARLY = 3
+LAG_FAR = 1
+LAG_USE = 2
+MIX = 3
 MIB = 1024 * 1024
 
 
@@ -29,6 +32,10 @@
 def behind(seq, d):
     y, x = seq // SIDE, seq % SIDE
     return ((y + SIDE - d // SIDE) % SIDE) * SIDE + (x + SIDE - d % SIDE) % SIDE
+
+
+def each_group(step):
+    loop(1, GROUPS, lambda d: step(d * MIX % GROUPS))
 
 
 def loop(low, high, step):
@@ -109,7 +116,7 @@
                 (r.value_weight, r.wv),
                 (r.queries, r.q),
                 (r.grad_ctx, r.go),
-                (r.neighbours, r.raw),
+                (r.neighbours.at[:, ret], r.raw.at[pl.ds(2 * ret, 2)]),
             )
         )
     ]
@@ -140,72 +147,87 @@
     to_source = pltpu.make_async_copy(r.source_v, r.source, r.scalar_sem.at[1])
     to_source.start()
 
+    def id_copy(d, dest, slot):
+        return remote(r.wanted, r.served.at[slot], r.id_send.at[d], r.id_recv.at[d], (dest, ret))
+
+    def raw_copy(d, dest, slot):
+        return remote(
+            r.neighbours.at[:, dest],
+            r.raw.at[pl.ds(2 * slot, 2)],
+            r.raw_send.at[d],
+            r.raw_recv.at[d],
+            (seq, dest),
+        )
+
+    greeted()
+    loop(1, RETS, lambda d: raw_copy(d, (ret + d) % RETS, ret).start())
+    loop(1, GROUPS, lambda d: id_copy(d, ahead(seq, d), seq).start())
+    r.served[seq] = wanted
+    for j in range(BLOCKS):
+        up_load(j).wait()
+        down_load(j).wait()
+    loop(1, GROUPS, lambda d: id_copy(d, ahead(seq, d), behind(seq, d)).wait())
+    to_scalar = pltpu.make_async_copy(r.served, r.served_s, r.scalar_sem.at[0])
+    to_scalar.start()
     loads[4].wait()
+    loop(1, RETS, lambda d: raw_copy(d, (ret + d) % RETS, (ret + RETS - d) % RETS).wait())
+
     inputs = r.raw[...].reshape(-1, feat).astype(jnp.float32)
     normed = inputs * lax.rsqrt(jnp.mean(inputs * inputs, axis=-1, keepdims=True) + 1e-06)
     r.normed[...] = normed.astype(jnp.bfloat16)
-    r.encoding[...] = inputs
-
-    def feed(j):
-        up_load(j).wait()
-        hidden = jax.nn.gelu(dot(r.normed[...], r.up_w[j])).astype(jnp.bfloat16)
-        down_load(j).wait()
-        r.encoding[...] += dot(hidden, r.down_w[j])
-
-    loop(0, BLOCKS, feed)
-    r.enc[...] = r.encoding[...].astype(jnp.bfloat16).reshape(r.enc.shape)
+    before = dot(r.normed[...], r.up_w[0])
+    encoding = None
+    for j in range(BLOCKS):
+        following = dot(r.normed[...], r.up_w[j + 1]) if j < BLOCKS - 1 else None
+        added = dot(jax.nn.gelu(before).astype(jnp.bfloat16), r.down_w[j])
+        encoding = added if encoding is None else encoding + added
+        before = following
+    encoding = r.raw[...].reshape(-1, feat).astype(jnp.float32) + encoding
+    r.table[...] = encoding.astype(jnp.bfloat16).reshape(r.table.shape)
     to_source.wait()
-    greeted()
-
-    def id_copy(d, dest, slot):
-        return remote(r.wanted, r.served.at[slot], r.id_send.at[d], r.id_recv.at[d], (dest, ret))
-
-    def slice_copy(d, dest, slot):
-        return remote(
-            r.enc.at[:, dest],
-            r.table.at[pl.ds(2 * slot, 2)],
-            r.raw_send.at[d],
-            r.raw_recv.at[d],
-            (seq, dest),
-        )
-
-    loop(1, RETS, lambda d: slice_copy(d, (ret + d) % RETS, ret).start())
-    loop(1, GROUPS, lambda d: id_copy(d, ahead(seq, d), seq).start())
-    r.served[seq] = wanted
-    for k in range(2):
-        r.table[2 * ret + k] = r.enc[k, ret]
-    loop(1, GROUPS, lambda d: id_copy(d, ahead(seq, d), behind(seq, d)).wait())
-    to_scalar = pltpu.make_async_copy(r.served, r.served_s, r.scalar_sem.at[0])
-    to_scalar.start()
     to_scalar.wait()
-    loop(1, RETS, lambda d: slice_copy(d, (ret + d) % RETS, (ret + RETS - d) % RETS).wait())
 
     def asked(s, k):
         return r.served_s[s, 0, seq * CAP + k]
 
-    def seq_copy(d, dest, slot):
-        return remote(
-            r.leaving.at[dest], r.arrived.at[slot], r.seq_send.at[d], r.seq_recv.at[d], (dest, ret)
-        )
-
-    def serve(d):
-        dest = ahead(seq, d)
-        for k in range(CAP):
-            r.leaving[dest, k] = r.table[jnp.maximum(asked(dest, k), 0)]
-        seq_copy(d, dest, seq).start()
-
-    loop(1, GROUPS, serve)
+    def seq_copy(e, d, dest, slot):
+        places = pl.ds(0, 2) if e == 0 else pl.ds(2, CAP - 2)
+        return remote(
+            r.leaving.at[dest, places],
+            (r.arrived if e == 0 else r.arrived_third).at[slot],
+            r.seq_send.at[e, d],
+            r.seq_recv.at[e, d],
+            (dest, ret),
+        )
+
+    def serve(e):
+        def one(d):
+            dest = ahead(seq, d)
+            for k in ((0, 1), range(2, CAP))[e]:
+                r.leaving[dest, k] = r.table[jnp.maximum(asked(dest, k), 0)]
+            seq_copy(e, d, dest, seq).start()
+
+        each_group(one)
+
+    serve(0)
+    serve(1)
     for k in range(CAP):
-        r.arrived[seq, k] = r.table[jnp.maximum(asked(seq, k), 0)]
-    loop(1, GROUPS, lambda d: seq_copy(d, ahead(seq, d), behind(seq, d)).wait())
+        mine = r.table[jnp.maximum(asked(seq, k), 0)]
+        if k < 2:
+            r.arrived[seq, k] = mine
+        else:
+            r.arrived_third[seq, k - 2] = mine
+
+    def first(i):
+        at = r.position[i]
+        r.own[i] = r.arrived[at // CAP, jnp.minimum(at % CAP, 1)]
 
     def compact(i):
         at = r.position[i]
-        r.own[i] = r.arrived[at // CAP, at % CAP]
-
-    loop(0, requests, compact)
-    for i in range(4):
-        loads[i].wait()
+        group, place = at // CAP, at % CAP
+        r.own[i] = jnp.where(
+            place < 2, r.arrived[group, jnp.minimum(place, 1)], r.arrived_third[group, 0]
+        )
 
     def rows(g, h):
         return pl.ds(g * size + h * half, half)
@@ -388,17 +410,34 @@
         def _():
             step(g)
 
-    for g in range(EARLY):
+    each_group(lambda d: seq_copy(0, d, ahead(seq, d), behind(seq, d)).wait())
+    loop(0, size, first)
+    send_own(0)
+    for i in range(4):
+        loads[i].wait()
+    each_group(lambda d: seq_copy(1, d, ahead(seq, d), behind(seq, d)).wait())
+    loop(size, requests, compact)
+    for g in range(1, EARLY):
         send_own(g)
 
+    def tock(t):
+        for p in range(2):
+            begin = 4 + p * STEPS
+            at_step(t - begin - 5, lambda g: finish(p, g))
+            at_step(t - begin - 3, lambda g: add_far(p, g))
+            at_step(t - begin - 1, lambda g: merge_all(p, g))
+            at_step(t - begin, lambda g: project(p, g))
+
     def tick(t):
+        at_step(t, pass_on)
         at_step(t + EARLY, send_own)
-        at_step(t, pass_on)
-        at_step(t - 1, pass_far)
-        at_step(t - 2, settle)
-        at_step(t - 2, compute)
-
-    loop(0, STEPS + 2, tick)
+        at_step(t - LAG_FAR, pass_far)
+        at_step(t - LAG_USE, settle)
+        at_step(t - LAG_USE, compute)
+        tock(t)
+
+    phase = STEPS + LAG_USE
+    loop(0, phase, tick)
 
     y, x = seq // SIDE, seq % SIDE
     each = feat // GROUPS
@@ -468,21 +507,16 @@
                 r.leaving[dest, k, :, cols[p]] = r.total[r.source[0, dest * CAP + k], :, cols[p]]
             back_copy(p, d, dest, seq).start()
 
-        loop(1, GROUPS, give)
+        each_group(give)
         for k in range(CAP):
             r.arrived_b[seq, k, :, cols[p]] = r.total[r.source[0, seq * CAP + k], :, cols[p]]
 
-    def tock(t):
-        for p in range(2):
-            begin = p * STEPS
-            at_step(t - begin - 5, lambda g: finish(p, g))
-            at_step(t - begin - 3, lambda g: add_far(p, g))
-            at_step(t - begin - 1, lambda g: merge_all(p, g))
-            at_step(t - begin, lambda g: project(p, g))
-        pl.when(t == STEPS)(w_middle)
-        pl.when(t == STEPS + 4)(lambda: give_back(0))
-
-    loop(0, 2 * STEPS + 5, tock)
+    def last_tick(t):
+        tock(t)
+        pl.when(t == 4 + STEPS + 4)(w_middle)
+        pl.when(t == 4 + STEPS + 5)(lambda: give_back(0))
+
+    loop(phase, 4 + 2 * STEPS + 5, last_tick)
     give_back(1)
 
     row = lax.broadcasted_iota(jnp.int32, r.pick.shape, 0)
@@ -506,7 +540,7 @@
         )
 
     def go_home(p):
-        loop(1, GROUPS, lambda d: back_copy(p, d, ahead(seq, d), behind(seq, d)).wait())
+        each_group(lambda d: back_copy(p, d, ahead(seq, d), behind(seq, d)).wait())
         arrived = r.arrived_b[:, :, :, cols[p]]
         summed = dot(r.pick[...], arrived.reshape(r.pick.shape[1], arrived.shape[-1]))
         r.table[:, :, cols[p]] = summed.astype(jnp.bfloat16).reshape(
@@ -536,12 +570,17 @@
             copy.wait()
 
 
+def picked_rows(r, g, count):
+    first = g * (r.own.shape[0] // STEPS)
+    return r.picked[pl.ds(first, count)].reshape(count * 128, r.wk.shape[0])
+
+
 def attend(r, g, size):
     feat, width = r.wk.shape
     heads = width // HD
     spans = size // 2
     scale = 1.0 / math.sqrt(HD)
-    rows = r.picked[pl.ds(g * size, size)].reshape(size * 128, feat)
+    rows = picked_rows(r, g, size)
     r.keys[...] = dot(rows, r.wk[...]).astype(jnp.bfloat16)
     r.values[...] = dot(rows, r.wv[...]).astype(jnp.bfloat16)
     gkeys, gvalues = r.up_w.at[g, : size * 128], r.down_w.at[g, :, :width]
@@ -563,18 +602,24 @@
             r.gq[tok, col] = dot(m, r.keys[row, col]).astype(jnp.bfloat16)
             gkeys[row, col] = dot(m, r.q[tok, col], TN).astype(jnp.bfloat16)
             gvalues[row, col] = dot(p, r.go[tok, col], TN).astype(jnp.bfloat16)
-    add_k = dot(rows, gkeys[...], TN)
-    add_v = dot(rows, gvalues[...], TN)
-
-    @pl.when(g == 0)
+
+    @pl.when(g % 2 == 1)
     def _():
-        r.acc_k[...] = add_k
-        r.acc_v[...] = add_v
-
-    @pl.when(g > 0)
-    def _():
-        r.acc_k[...] += add_k
-        r.acc_v[...] += add_v
+        pair = picked_rows(r, g - 1, 2 * size)
+        gk = r.up_w[pl.ds(g - 1, 2), : size * 128].reshape(-1, width)
+        gv = r.down_w[pl.ds(g - 1, 2), :, :width].reshape(-1, width)
+        add_k = dot(pair, gk, TN)
+        add_v = dot(pair, gv, TN)
+
+        @pl.when(g == 1)
+        def _():
+            r.acc_k[...] = add_k
+            r.acc_v[...] = add_v
+
+        @pl.when(g > 1)
+        def _():
+            r.acc_k[...] += add_k
+            r.acc_v[...] += add_v
 
 
 def fused(
@@ -625,14 +670,13 @@
         position=pltpu.SMEM((requests,), jnp.int32),
         served=pltpu.VMEM((GROUPS, 8, 128), jnp.int32),
         served_s=pltpu.SMEM((GROUPS, 8, 128), jnp.int32),
-        raw=pltpu.VMEM((2, RETS, 16, feat), bf),
-        enc=pltpu.VMEM((2, RETS, 16, feat), bf),
+        raw=pltpu.VMEM((2 * RETS, 16, feat), bf),
         normed=pltpu.VMEM((2 * RETS * 16, feat), bf),
-        encoding=pltpu.VMEM((2 * RETS * 16, feat), f32),
         up_w=pltpu.VMEM((BLOCKS, feat, ffe // BLOCKS), bf),
         down_w=pltpu.VMEM((BLOCKS, ffe // BLOCKS, feat), bf),
         table=pltpu.VMEM((2 * RETS, 16, feat), bf),
-        arrived=pltpu.VMEM(slots, bf),
+        arrived=pltpu.VMEM((GROUPS, 2, 16, feat), bf),
+        arrived_third=pltpu.VMEM((GROUPS, CAP - 2, 16, feat), bf),
         leaving=pltpu.VMEM(slots, bf),
         own=pltpu.VMEM(chunk, bf),
         picked=pltpu.VMEM((requests, RETS, 16, feat), bf),
@@ -668,7 +712,7 @@
     for name, shape in dict(
         id=(GROUPS,),
         raw=(RETS,),
-        seq=(GROUPS,),
+        seq=(2, GROUPS),
         up=(STEPS, 2),
         dn=(STEPS, 2),
         far=(STEPS, 2),

time: 141 us -> 131 us (0.929)
  Pallas kernels: 140 us -> 130 us
    pallas_call x1, Pallas kernels: 137 us -> 128 us  [fused(): pl.pallas_call(functools.partial(kernel, names), out_shape=tuple((jax.Sha...]
where the time goes in v4:
time: 131 us
  Pallas kernels  130 us (99%)
    pallas_call x1, Pallas kernels, fused(): pl.pallas_call(functools.partial(kernel, names), out_shape=tuple((jax.Sha...  128 us

profile of v4, /device:TPU:1, one launch (start us, length us, event | category | flops | bytes accessed | tf_op | source)
XLA Modules:
  0.0 130.9 jit_solution(13683867940404073425)
XLA Ops:
  0.6 127.6 %fused.1 = (bf16[768,512]{1,0:T(8,128)(2,1)}, bf16[768,512]{1,0:T(8,128)(2,1)}, bf16[2,8,16,896]{3,2,1,0:T(8,128)(2,1)}, f32[56,512]{1,0:T(8,128)}, f32[56,512]{1,0:T(8,128)}) custom-call(bf16[768,512]{1,0:T(8,128)(2,1)} %refs_0_.1, bf16[768,512]{1,0:T(8,128)(2,1)} %refs_1_.1, bf16[2,8,16,896]{3,2,1,0:T(8,128)(2,1)} %bitcast.4, bf16[896,3584]{1,0:T(8,128)(2,1)} %refs_3_.1, ...), custom_call_target="tpu_custom_call" | custom-call | tf_op jit(solution)/shard_map/fused/pallas_call | solution.py:732
  128.3 2.6 %deliver.1 = (bf16[768,512]{1,0:T(8,128)(2,1)}, bf16[768,512]{1,0:T(8,128)(2,1)}, bf16[2,8,16,896]{3,2,1,0:T(8,128)(2,1)}, f32[56,512]{1,0:T(8,128)}, f32[56,512]{1,0:T(8,128)}) custom-call(bf16[768,512]{1,0:T(8,128)(2,1)} %get-tuple-element.15.refs_0_, bf16[768,512]{1,0:T(8,128)(2,1)} %get-tuple-element.16.refs_1_, ...), custom_call_target="tpu_custom_call" | custom-call | tf_op jit(solution)/shard_map/deliver/pallas_call | solution.py:776

commit v5 on v4

--- a/solution.py
+++ b/solution.py
@@ -18,8 +18,7 @@
 BLOCKS = 7
 CUT = 512
 EARLY = 3
-LAG_FAR = 1
-LAG_USE = 2
+LAG_PART = 1
 MIX = 3
 MIB = 1024 * 1024
 
@@ -58,6 +57,10 @@
     loop(1, GROUPS, to_seq)
     loop(1, RETS, to_ret)
     return lambda: pl.semaphore_wait(barrier, GROUPS + RETS - 2)
+
+
+def drain(like, sem):
+    pltpu.make_async_copy(like, like, sem).wait()
 
 
 def remote(src, dst, send, recv, to):
@@ -99,13 +102,13 @@
     def up_load(j):
         width = r.up_w.shape[-1]
         return pltpu.make_async_copy(
-            r.up_weight.at[:, pl.ds(j * width, width)], r.up_w.at[j], r.up_sem.at[j]
+            r.up_weight.at[:, pl.ds(j * width, width)], r.up_w.at[j], r.up_sem
         )
 
     def down_load(j):
         depth = r.down_w.shape[1]
         return pltpu.make_async_copy(
-            r.down_weight.at[pl.ds(j * depth, depth)], r.down_w.at[j], r.down_sem.at[j]
+            r.down_weight.at[pl.ds(j * depth, depth)], r.down_w.at[j], r.down_sem
         )
 
     loads = [
@@ -121,11 +124,6 @@
         )
     ]
     loads[4].start()
-    for j in range(BLOCKS):
-        up_load(j).start()
-        down_load(j).start()
-    for i in range(4):
-        loads[i].start()
 
     greeted = greet(seq, ret)
 
@@ -148,29 +146,36 @@
     to_source.start()
 
     def id_copy(d, dest, slot):
-        return remote(r.wanted, r.served.at[slot], r.id_send.at[d], r.id_recv.at[d], (dest, ret))
+        return remote(r.wanted, r.served.at[slot], r.id_send, r.id_recv, (dest, ret))
 
     def raw_copy(d, dest, slot):
         return remote(
             r.neighbours.at[:, dest],
             r.raw.at[pl.ds(2 * slot, 2)],
-            r.raw_send.at[d],
-            r.raw_recv.at[d],
+            r.raw_send,
+            r.raw_recv,
             (seq, dest),
         )
 
     greeted()
     loop(1, RETS, lambda d: raw_copy(d, (ret + d) % RETS, ret).start())
     loop(1, GROUPS, lambda d: id_copy(d, ahead(seq, d), seq).start())
+    for j in range(BLOCKS):
+        up_load(j).start()
+        down_load(j).start()
     r.served[seq] = wanted
-    for j in range(BLOCKS):
-        up_load(j).wait()
-        down_load(j).wait()
-    loop(1, GROUPS, lambda d: id_copy(d, ahead(seq, d), behind(seq, d)).wait())
+    drain(r.served.at[pl.ds(0, GROUPS - 1)], r.id_recv)
+    drain(r.served.at[pl.ds(0, GROUPS - 1)], r.id_send)
     to_scalar = pltpu.make_async_copy(r.served, r.served_s, r.scalar_sem.at[0])
     to_scalar.start()
     loads[4].wait()
-    loop(1, RETS, lambda d: raw_copy(d, (ret + d) % RETS, (ret + RETS - d) % RETS).wait())
+    drain(r.raw.at[pl.ds(0, 2 * (RETS - 1))], r.raw_recv)
+    drain(r.raw.at[pl.ds(0, 2 * (RETS - 1))], r.raw_send)
+
+    drain(r.up_w, r.up_sem)
+    drain(r.down_w, r.down_sem)
+    for i in range(4):
+        loads[i].start()
 
     inputs = r.raw[...].reshape(-1, feat).astype(jnp.float32)
     normed = inputs * lax.rsqrt(jnp.mean(inputs * inputs, axis=-1, keepdims=True) + 1e-06)
@@ -195,8 +200,8 @@
         return remote(
             r.leaving.at[dest, places],
             (r.arrived if e == 0 else r.arrived_third).at[slot],
-            r.seq_send.at[e, d],
-            r.seq_recv.at[e, d],
+            r.seq_send.at[e],
+            r.seq_recv.at[e],
             (dest, ret),
         )
 
@@ -236,7 +241,7 @@
         return remote(
             r.own.at[rows(g, h)],
             r.picked.at[rows(g, h), 2 * held + core],
-            r.up_send.at[g, h],
+            r.up_send,
             r.up_recv.at[g, h],
             up_to,
         )
@@ -245,7 +250,7 @@
         return remote(
             r.own.at[rows(g, h)],
             r.picked.at[rows(g, h), 2 * held + core],
-            r.dn_send.at[g, h],
+            r.dn_send,
             r.dn_recv.at[g, h],
             down_to,
         )
@@ -254,8 +259,8 @@
         return remote(
             r.picked.at[rows(g, h), 2 * held + core],
             r.picked.at[rows(g, h), 2 * held + core],
-            r.far_send.at[g, h],
-            r.far_recv.at[g, h],
+            r.far_send,
+            r.far_recv.at[g],
             down_to if h else up_to,
         )
 
@@ -265,8 +270,8 @@
         return remote(
             r.own.at[whole] if o == 0 else source,
             source,
-            r.sib_send.at[g, o],
-            r.sib_recv.at[g, o],
+            r.sib_send,
+            r.sib_recv.at[g],
             sibling,
         )
 
@@ -295,20 +300,12 @@
         across(g, 2, above, core).start()
 
     def pass_far(g):
-        relay(g, 0, facing).wait_recv()
-        relay(g, 1, facing).wait_recv()
+        drain(r.own.at[pl.ds(0, size)], r.far_recv.at[g])
         across(g, 3, facing, core).start()
 
     def settle(g):
-        for h in range(2):
-            own_up(g, h, z).wait_send()
-            own_down(g, h, z).wait_send()
-            relay(g, h, above if h else below).wait_send()
         keep(g).wait()
-        across(g, 0, z, 1 - core).wait()
-        across(g, 1, below, 1 - core).wait()
-        across(g, 2, above, 1 - core).wait()
-        across(g, 3, facing, 1 - core).wait()
+        drain(r.picked.at[pl.ds(0, size), pl.ds(0, SIDE)], r.sib_recv.at[g])
 
     cols = (pl.ds(0, CUT), pl.ds(CUT, feat - CUT))
 
@@ -317,31 +314,29 @@
         return remote(
             r.part.at[whole, (z + o) % SIDE, 1 - core, :, cols[p]],
             r.sib.at[o, whole, :, cols[p]],
-            r.swap_send.at[p, g, o],
-            r.swap_recv.at[p, g, o],
+            r.swap_send.at[p],
+            r.swap_recv.at[p, g],
             sibling,
         )
 
-    def ring_copy(name, dst, at, to):
-        send, recv = getattr(r, name + "_send"), getattr(r, name + "_recv")
+    def ring_copy(send, recv, dst, at, to):
 
         def copy(p, g, h):
             return remote(
                 r.part.at[rows(g, h), at, core, :, cols[p]],
                 dst.at[rows(g, h), :, cols[p]],
-                send.at[p, g, h],
-                recv.at[p, g, h],
+                send.at[p],
+                recv.at[p, g],
                 to(h),
             )
 
         return copy
 
-    far_copy = ring_copy("rfar", r.far, facing, lambda h: down_to if h else up_to)
-    up_copy = ring_copy("rup", r.near_up, above, lambda h: up_to)
-    down_copy = ring_copy("rdn", r.near_down, below, lambda h: down_to)
+    far_copy = ring_copy(r.rfar_send, r.rfar_recv, r.far, facing, lambda h: down_to if h else up_to)
+    up_copy = ring_copy(r.near_send, r.near_recv, r.near_up, above, lambda h: up_to)
+    down_copy = ring_copy(r.near_send, r.near_recv, r.near_down, below, lambda h: down_to)
 
     def merge(p, g, o):
-        swap(p, g, o).wait_recv()
         at = (z + o) % SIDE
         whole = pl.ds(g * size, size)
         mine = r.part[whole, at, core, :, cols[p]].astype(jnp.float32)
@@ -349,6 +344,7 @@
         r.part[whole, at, core, :, cols[p]] = (mine + other).astype(jnp.bfloat16)
 
     def merge_all(p, g):
+        drain(r.sib.at[:, pl.ds(0, size), :, cols[p]], r.swap_recv.at[p, g])
         merge(p, g, 2)
         far_copy(p, g, 0).start()
         far_copy(p, g, 1).start()
@@ -359,8 +355,8 @@
         merge(p, g, 0)
 
     def add_far(p, g):
+        drain(r.far.at[pl.ds(0, size), :, cols[p]], r.rfar_recv.at[p, g])
         for h in range(2):
-            far_copy(p, g, h).wait_recv()
             at = below if h else above
             mine = r.part[rows(g, h), at, core, :, cols[p]].astype(jnp.float32)
             other = r.far[rows(g, h), :, cols[p]].astype(jnp.float32)
@@ -368,21 +364,13 @@
             (down_copy if h else up_copy)(p, g, h).start()
 
     def finish(p, g):
-        for h in range(2):
-            up_copy(p, g, h).wait_recv()
-            down_copy(p, g, h).wait_recv()
+        drain(r.sib.at[pl.ds(0, 2), pl.ds(0, size), :, cols[p]], r.near_recv.at[p, g])
         whole = pl.ds(g * size, size)
         r.total[whole, :, cols[p]] = (
             r.part[whole, z, core, :, cols[p]].astype(jnp.float32)
             + r.near_up[whole, :, cols[p]].astype(jnp.float32)
             + r.near_down[whole, :, cols[p]].astype(jnp.float32)
         ).astype(jnp.bfloat16)
-        for o in range(4):
-            swap(p, g, o).wait_send()
-        for h in range(2):
-            far_copy(p, g, h).wait_send()
-            up_copy(p, g, h).wait_send()
-            down_copy(p, g, h).wait_send()
 
     def project(p, g):
         gk, gv = r.up_w[g, : size * 128, :], r.down_w[g, :, : r.wk.shape[1]]
@@ -396,12 +384,12 @@
     def result_copies(g):
         tokens = pl.ds(g * (size * 32), size * 32)
         return (
-            pltpu.make_async_copy(r.ctx.at[tokens], r.context.at[tokens], r.out_sem.at[g, 0]),
-            pltpu.make_async_copy(r.gq.at[tokens], r.grad_query.at[tokens], r.out_sem.at[g, 1]),
+            pltpu.make_async_copy(r.ctx.at[tokens], r.context.at[tokens], r.out_sem.at[0]),
+            pltpu.make_async_copy(r.gq.at[tokens], r.grad_query.at[tokens], r.out_sem.at[1]),
         )
 
     def compute(g):
-        attend(r, g, size)
+        weight_grads(r, g, size)
         for copy in result_copies(g):
             copy.start()
 
@@ -410,34 +398,38 @@
         def _():
             step(g)
 
-    each_group(lambda d: seq_copy(0, d, ahead(seq, d), behind(seq, d)).wait())
+    drain(r.arrived.at[pl.ds(0, GROUPS - 1)], r.seq_recv.at[0])
+    drain(r.arrived.at[pl.ds(0, GROUPS - 1)], r.seq_send.at[0])
     loop(0, size, first)
     send_own(0)
+    pass_on(0)
     for i in range(4):
         loads[i].wait()
-    each_group(lambda d: seq_copy(1, d, ahead(seq, d), behind(seq, d)).wait())
+    drain(r.arrived_third.at[pl.ds(0, GROUPS - 1)], r.seq_recv.at[1])
+    drain(r.arrived_third.at[pl.ds(0, GROUPS - 1)], r.seq_send.at[1])
     loop(size, requests, compact)
-    for g in range(1, EARLY):
-        send_own(g)
 
     def tock(t):
         for p in range(2):
-            begin = 4 + p * STEPS
+            begin = LAG_PART + p * STEPS
             at_step(t - begin - 5, lambda g: finish(p, g))
             at_step(t - begin - 3, lambda g: add_far(p, g))
             at_step(t - begin - 1, lambda g: merge_all(p, g))
             at_step(t - begin, lambda g: project(p, g))
 
     def tick(t):
-        at_step(t, pass_on)
+        at_step(t + 1, pass_on)
         at_step(t + EARLY, send_own)
-        at_step(t - LAG_FAR, pass_far)
-        at_step(t - LAG_USE, settle)
-        at_step(t - LAG_USE, compute)
+        settle(t)
+        attend(r, t, size)
+        at_step(t + 1, pass_far)
+        compute(t)
         tock(t)
 
-    phase = STEPS + LAG_USE
-    loop(0, phase, tick)
+    for g in range(1, EARLY):
+        send_own(g)
+    pass_far(0)
+    loop(0, STEPS, tick)
 
     y, x = seq // SIDE, seq % SIDE
     each = feat // GROUPS
@@ -495,8 +487,8 @@
         return remote(
             r.leaving.at[dest, :, :, cols[p]],
             r.arrived_b.at[slot, :, :, cols[p]],
-            r.back_send.at[p, d],
-            r.back_recv.at[p, d],
+            r.back_send.at[p],
+            r.back_recv.at[p],
             (dest, ret),
         )
 
@@ -513,10 +505,10 @@
 
     def last_tick(t):
         tock(t)
-        pl.when(t == 4 + STEPS + 4)(w_middle)
-        pl.when(t == 4 + STEPS + 5)(lambda: give_back(0))
-
-    loop(phase, 4 + 2 * STEPS + 5, last_tick)
+        pl.when(t == LAG_PART + STEPS + 5)(w_middle)
+        pl.when(t == LAG_PART + STEPS + 5)(lambda: give_back(0))
+
+    loop(STEPS, LAG_PART + 2 * STEPS + 5, last_tick)
     give_back(1)
 
     row = lax.broadcasted_iota(jnp.int32, r.pick.shape, 0)
@@ -534,13 +526,13 @@
         return remote(
             r.table.at[pl.ds(2 * dest, 2), :, cols[p]],
             r.home.at[:, slot, :, cols[p]],
-            r.home_send.at[p, d],
-            r.home_recv.at[p, d],
+            r.home_send.at[p],
+            r.home_recv.at[p],
             (seq, dest),
         )
 
     def go_home(p):
-        each_group(lambda d: back_copy(p, d, ahead(seq, d), behind(seq, d)).wait())
+        drain(r.arrived_b.at[pl.ds(0, GROUPS - 1), :, :, cols[p]], r.back_recv.at[p])
         arrived = r.arrived_b[:, :, :, cols[p]]
         summed = dot(r.pick[...], arrived.reshape(r.pick.shape[1], arrived.shape[-1]))
         r.table[:, :, cols[p]] = summed.astype(jnp.bfloat16).reshape(
@@ -560,14 +552,19 @@
         r.gv_out[:, wide * h : wide * h + wide] = summed[each:]
     go_home(1)
     for p in range(2):
-        loop(
-            1,
-            RETS,
-            lambda d: home_copy(p, d, (ret + d) % RETS, (ret + RETS - d) % RETS).wait(),
-        )
-    for g in range(STEPS):
-        for copy in result_copies(g):
-            copy.wait()
+        sent_home = r.home.at[:, pl.ds(0, RETS - 1), :, cols[p]]
+        drain(sent_home, r.home_recv.at[p])
+        drain(sent_home, r.home_send.at[p])
+        drain(r.arrived_b.at[pl.ds(0, GROUPS - 1), :, :, cols[p]], r.back_send.at[p])
+        drain(r.sib.at[:, :, :, cols[p]], r.swap_send.at[p])
+        drain(r.far.at[:, :, cols[p]], r.rfar_send.at[p])
+        drain(r.sib.at[pl.ds(0, 2), :, :, cols[p]], r.near_send.at[p])
+    drain(r.own, r.up_send)
+    drain(r.own, r.dn_send)
+    drain(r.own, r.far_send)
+    drain(r.picked.at[:, pl.ds(0, SIDE)], r.sib_send)
+    drain(r.ctx, r.out_sem.at[0])
+    drain(r.gq, r.out_sem.at[1])
 
 
 def picked_rows(r, g, count):
@@ -602,6 +599,10 @@
             r.gq[tok, col] = dot(m, r.keys[row, col]).astype(jnp.bfloat16)
             gkeys[row, col] = dot(m, r.q[tok, col], TN).astype(jnp.bfloat16)
             gvalues[row, col] = dot(p, r.go[tok, col], TN).astype(jnp.bfloat16)
+
+
+def weight_grads(r, g, size):
+    width = r.wk.shape[1]
 
     @pl.when(g % 2 == 1)
     def _():
@@ -702,32 +703,31 @@
         w_half=pltpu.VMEM((2, SIDE) + block, bf),
         w_end=pltpu.VMEM((2, SIDE) + block, bf),
         pick=pltpu.VMEM((2 * RETS * 16, GROUPS * CAP * 16), bf),
-        up_sem=dma((BLOCKS,)),
-        down_sem=dma((BLOCKS,)),
+        up_sem=dma,
+        down_sem=dma,
         load_sem=dma((5,)),
         scalar_sem=dma((2,)),
         keep_sem=dma((STEPS,)),
-        out_sem=dma((STEPS, 2)),
+        out_sem=dma((2,)),
     )
-    for name, shape in dict(
-        id=(GROUPS,),
-        raw=(RETS,),
-        seq=(2, GROUPS),
-        up=(STEPS, 2),
-        dn=(STEPS, 2),
-        far=(STEPS, 2),
-        sib=(STEPS, 4),
-        swap=(2, STEPS, 4),
-        rfar=(2, STEPS, 2),
-        rup=(2, STEPS, 2),
-        rdn=(2, STEPS, 2),
-        w=(2, SIDE),
-        w2=(2, SIDE),
-        back=(2, GROUPS),
-        home=(2, RETS),
+    for name, (send, recv) in dict(
+        id=((), ()),
+        raw=((), ()),
+        seq=((2,), (2,)),
+        up=((), (STEPS, 2)),
+        dn=((), (STEPS, 2)),
+        far=((), (STEPS,)),
+        sib=((), (STEPS,)),
+        swap=((2,), (2, STEPS)),
+        rfar=((2,), (2, STEPS)),
+        near=((2,), (2, STEPS)),
+        w=((2, SIDE), (2, SIDE)),
+        w2=((2, SIDE), (2, SIDE)),
+        back=((2,), (2,)),
+        home=((2,), (2,)),
     ).items():
-        scratch[name + "_send"] = dma(shape)
-        scratch[name + "_recv"] = dma(shape)
+        scratch[name + "_send"] = dma(send) if send else dma
+        scratch[name + "_recv"] = dma(recv) if recv else dma
     names = tuple(ins) + tuple(outs) + tuple(scratch)
     return pl.pallas_call(
         functools.partial(kernel, names),

time: 131 us -> 126 us (0.962)
  Pallas kernels: 130 us -> 125 us
    pallas_call x1, Pallas kernels: 128 us -> 122 us  [fused(): pl.pallas_call(functools.partial(kernel, names), out_shape=tuple((jax.Sha...]
where the time goes in v5:
time: 126 us
  Pallas kernels  125 us (99%)
    pallas_call x1, Pallas kernels, fused(): pl.pallas_call(functools.partial(kernel, names), out_shape=tuple((jax.Sha...  122 us
    pallas_call x1, Pallas kernels, deliver(): pl.pallas_call(deliver_kernel, out_shape=tuple((jax.ShapeDtypeStruct(a.sh...  2.57 us

profile of v5, /device:TPU:1, one launch (start us, length us, event | category | flops | bytes accessed | tf_op | source)
XLA Modules:
  0.0 125.7 jit_solution(9478102076790062967)
XLA Ops:
  0.6 122.5 %fused.1 = (bf16[768,512]{1,0:T(8,128)(2,1)}, bf16[768,512]{1,0:T(8,128)(2,1)}, bf16[2,8,16,896]{3,2,1,0:T(8,128)(2,1)}, f32[56,512]{1,0:T(8,128)}, f32[56,512]{1,0:T(8,128)}) custom-call(bf16[768,512]{1,0:T(8,128)(2,1)} %refs_0_.1, bf16[768,512]{1,0:T(8,128)(2,1)} %refs_1_.1, bf16[2,8,16,896]{3,2,1,0:T(8,128)(2,1)} %bitcast.4, bf16[896,3584]{1,0:T(8,128)(2,1)} %refs_3_.1, ...), custom_call_target="tpu_custom_call" | custom-call | tf_op jit(solution)/shard_map/fused/pallas_call | solution.py:732
  123.1 2.6 %deliver.1 = (bf16[768,512]{1,0:T(8,128)(2,1)}, bf16[768,512]{1,0:T(8,128)(2,1)}, bf16[2,8,16,896]{3,2,1,0:T(8,128)(2,1)}, f32[56,512]{1,0:T(8,128)}, f32[56,512]{1,0:T(8,128)}) custom-call(bf16[768,512]{1,0:T(8,128)(2,1)} %get-tuple-element.15.refs_0_, bf16[768,512]{1,0:T(8,128)(2,1)} %get-tuple-element.16.refs_1_, ...), custom_call_target="tpu_custom_call" | custom-call | tf_op jit(solution)/shard_map/deliver/pallas_call | solution.py:776

commit v6 on v5

--- a/solution.py
+++ b/solution.py
@@ -412,19 +412,19 @@
     def tock(t):
         for p in range(2):
             begin = LAG_PART + p * STEPS
-            at_step(t - begin - 5, lambda g: finish(p, g))
-            at_step(t - begin - 3, lambda g: add_far(p, g))
-            at_step(t - begin - 1, lambda g: merge_all(p, g))
+            at_step(t - begin - 6, lambda g: finish(p, g))
+            at_step(t - begin - 4, lambda g: add_far(p, g))
+            at_step(t - begin - 2, lambda g: merge_all(p, g))
             at_step(t - begin, lambda g: project(p, g))
 
     def tick(t):
         at_step(t + 1, pass_on)
         at_step(t + EARLY, send_own)
         settle(t)
+        tock(t)
         attend(r, t, size)
         at_step(t + 1, pass_far)
         compute(t)
-        tock(t)
 
     for g in range(1, EARLY):
         send_own(g)
@@ -505,10 +505,10 @@
 
     def last_tick(t):
         tock(t)
-        pl.when(t == LAG_PART + STEPS + 5)(w_middle)
-        pl.when(t == LAG_PART + STEPS + 5)(lambda: give_back(0))
-
-    loop(STEPS, LAG_PART + 2 * STEPS + 5, last_tick)
+        pl.when(t == LAG_PART + STEPS + 6)(w_middle)
+        pl.when(t == LAG_PART + STEPS + 6)(lambda: give_back(0))
+
+    loop(STEPS, LAG_PART + 2 * STEPS + 6, last_tick)
     give_back(1)
 
     row = lax.broadcasted_iota(jnp.int32, r.pick.shape, 0)

time: 126 us -> 123 us (0.976)
  Pallas kernels: 125 us -> 122 us
    pallas_call x1, Pallas kernels: 122 us -> 120 us  [fused(): pl.pallas_call(functools.partial(kernel, names), out_shape=tuple((jax.Sha...]
where the time goes in v6:
time: 123 us
  Pallas kernels  122 us (99%)
    pallas_call x1, Pallas kernels, fused(): pl.pallas_call(functools.partial(kernel, names), out_shape=tuple((jax.Sha...  120 us
    pallas_call x1, Pallas kernels, deliver(): pl.pallas_call(deliver_kernel, out_shape=tuple((jax.ShapeDtypeStruct(a.sh...  2.57 us

profile of v6, /device:TPU:1, one launch (start us, length us, event | category | flops | bytes accessed | tf_op | source)
XLA Modules:
  0.0 123.1 jit_solution(10356467101794522909)
XLA Ops:
  0.6 119.9 %fused.1 = (bf16[768,512]{1,0:T(8,128)(2,1)}, bf16[768,512]{1,0:T(8,128)(2,1)}, bf16[2,8,16,896]{3,2,1,0:T(8,128)(2,1)}, f32[56,512]{1,0:T(8,128)}, f32[56,512]{1,0:T(8,128)}) custom-call(bf16[768,512]{1,0:T(8,128)(2,1)} %refs_0_.1, bf16[768,512]{1,0:T(8,128)(2,1)} %refs_1_.1, bf16[2,8,16,896]{3,2,1,0:T(8,128)(2,1)} %bitcast.4, bf16[896,3584]{1,0:T(8,128)(2,1)} %refs_3_.1, ...), custom_call_target="tpu_custom_call" | custom-call | tf_op jit(solution)/shard_map/fused/pallas_call | solution.py:732
  120.5 2.6 %deliver.1 = (bf16[768,512]{1,0:T(8,128)(2,1)}, bf16[768,512]{1,0:T(8,128)(2,1)}, bf16[2,8,16,896]{3,2,1,0:T(8,128)(2,1)}, f32[56,512]{1,0:T(8,128)}, f32[56,512]{1,0:T(8,128)}) custom-call(bf16[768,512]{1,0:T(8,128)(2,1)} %get-tuple-element.15.refs_0_, bf16[768,512]{1,0:T(8,128)(2,1)} %get-tuple-element.16.refs_1_, ...), custom_call_target="tpu_custom_call" | custom-call | tf_op jit(solution)/shard_map/deliver/pallas_call | solution.py:776

commit v7 on v6

--- a/solution.py
+++ b/solution.py
@@ -505,7 +505,7 @@
 
     def last_tick(t):
         tock(t)
-        pl.when(t == LAG_PART + STEPS + 6)(w_middle)
+        pl.when(t == LAG_PART + STEPS + 4)(w_middle)
         pl.when(t == LAG_PART + STEPS + 6)(lambda: give_back(0))
 
     loop(STEPS, LAG_PART + 2 * STEPS + 6, last_tick)

time: 123 us -> 123 us (level)
  no operation moved by 1% of the time
where the time goes in v7:
time: 123 us; the launch traced here: 122 us
  Pallas kernels  122 us (99%)
    pallas_call x1, Pallas kernels, fused(): pl.pallas_call(functools.partial(kernel, names), out_shape=tuple((jax.Sha...  119 us
    pallas_call x1, Pallas kernels, deliver(): pl.pallas_call(deliver_kernel, out_shape=tuple((jax.ShapeDtypeStruct(a.sh...  2.57 us

profile of v7, /device:TPU:1, one launch (start us, length us, event | category | flops | bytes accessed | tf_op | source)
XLA Modules:
  0.0 122.4 jit_solution(12092667727996952483)
XLA Ops:
  0.6 119.2 %fused.1 = (bf16[768,512]{1,0:T(8,128)(2,1)}, bf16[768,512]{1,0:T(8,128)(2,1)}, bf16[2,8,16,896]{3,2,1,0:T(8,128)(2,1)}, f32[56,512]{1,0:T(8,128)}, f32[56,512]{1,0:T(8,128)}) custom-call(bf16[768,512]{1,0:T(8,128)(2,1)} %refs_0_.1, bf16[768,512]{1,0:T(8,128)(2,1)} %refs_1_.1, bf16[2,8,16,896]{3,2,1,0:T(8,128)(2,1)} %bitcast.4, bf16[896,3584]{1,0:T(8,128)(2,1)} %refs_3_.1, ...), custom_call_target="tpu_custom_call" | custom-call | tf_op jit(solution)/shard_map/fused/pallas_call | solution.py:732
  119.9 2.6 %deliver.1 = (bf16[768,512]{1,0:T(8,128)(2,1)}, bf16[768,512]{1,0:T(8,128)(2,1)}, bf16[2,8,16,896]{3,2,1,0:T(8,128)(2,1)}, f32[56,512]{1,0:T(8,128)}, f32[56,512]{1,0:T(8,128)}) custom-call(bf16[768,512]{1,0:T(8,128)(2,1)} %get-tuple-element.15.refs_0_, bf16[768,512]{1,0:T(8,128)(2,1)} %get-tuple-element.16.refs_1_, ...), custom_call_target="tpu_custom_call" | custom-call | tf_op jit(solution)/shard_map/deliver/pallas_call | solution.py:776
